TPU v7x, 512 devices: a whole 4x8x8 slice. The times are simulated.
512 devices in a mesh: dp: 32 (over x, z), table: 16 (over y, core).
Axes of the slice: x: 4, y: 8, z: 8, core: 2. Of those that a mesh axis runs over, the one named last changes fastest.
Arguments:
- query_out: bfloat16 [65536, 256], P(('dp', 'table')), may hold values from -15 to 15
- item_out: bfloat16 [65536, 256], P(('dp', 'table')), may hold values from -12 to 12
- pooled_query: bfloat16 [65536, 128], P(('dp', 'table')), may hold values from -6 to 6
- pooled_item: bfloat16 [65536, 128], P(('dp', 'table')), may hold values from -6 to 6
- w_query: bfloat16 [128, 256], replicated, may hold values from -0.5 to 0.5
- w_item: bfloat16 [128, 256], replicated, may hold values from -0.5 to 0.5
- pair_weight: float32 [65536], P(('dp', 'table')), may hold values from 1 to 8
- slot_owner: int32 [65536, 16, 1], P(('dp', 'table')), may hold values from 0 to 15; in each aligned block of 2048 rows (0 to 2047, 2048 to 4095, ..., all dimensions but the last counted through in order) at most 256 rows name the same one
- slot_row: int32 [65536, 16, 1], P(('dp', 'table')), may hold values from 0 to 4095
Outputs:
- grad_table: float32 [65536, 128], P('table')
- grad_w_query: float32 [128, 256], replicated
- grad_w_item: float32 [128, 256], replicated
Inputs may be any that keep to these rules, and one draw needn't show every extreme that they name: `slot_owner`: at most 256 of the 2048 slots of one device name the same owner, and some device has exactly 256 slots naming one owner.
All inputs are finite; a program needn't handle non-finite values.
Results may differ from a plain program's by a relative error of at most 0.023.
Values may be sent and summed in bfloat16 or wider, within the bound.
A program may use at most 64 MiB of HBM per device.

v0:
```python
import math

import jax
import jax.numpy as jnp
from jax import lax
from jax.sharding import PartitionSpec as P

R_DEV = 4096


def on_device(
    query_out,
    item_out,
    pooled_query,
    pooled_item,
    w_query,
    w_item,
    pair_weight,
    slot_owner,
    slot_row,
):
    pair_rows, tower_width = query_out.shape
    logit_scale = 1.0 / math.sqrt(tower_width)
    dp_index = lax.axis_index("dp")
    items_all = lax.all_gather(item_out, "dp", axis=0, tiled=True)
    group_size = items_all.shape[0]
    block_size = math.gcd(group_size, 1024)
    block_count = group_size // block_size
    item_blocks = items_all.reshape(block_count, block_size, tower_width)
    positive = dp_index * pair_rows + jnp.arange(pair_rows, dtype=jnp.int32)

    def logit_block(item_block):
        return logit_scale * lax.dot_general(
            item_block, query_out, (((1,), (1,)), ((), ())), preferred_element_type=jnp.float32
        )

    def stats_step(carry, item_block):
        run_max, run_sum = carry
        logits_t = logit_block(item_block)
        new_max = jnp.maximum(run_max, jnp.max(logits_t, axis=0))
        run_sum = run_sum * jnp.exp(run_max - new_max) + jnp.sum(
            jnp.exp(logits_t - new_max[None, :]), axis=0
        )
        return ((new_max, run_sum), None)

    start_carry = (jnp.full((pair_rows,), -1e30, jnp.float32), jnp.zeros((pair_rows,), jnp.float32))
    (row_max, row_total), _ = lax.scan(stats_step, start_carry, item_blocks)

    def weight_block(operands):
        item_block, block_start = operands
        logits_t = logit_block(item_block)
        softmax_prob = jnp.exp(logits_t - row_max[None, :]) / row_total[None, :]
        col_index = block_start + jnp.arange(block_size, dtype=jnp.int32)
        is_positive = (col_index[:, None] == positive[None, :]).astype(jnp.float32)
        return (pair_weight[None, :] * (softmax_prob - is_positive)).astype(jnp.bfloat16)

    block_starts = jnp.arange(block_count, dtype=jnp.int32) * block_size
    weights_t = lax.map(weight_block, (item_blocks, block_starts)).reshape(group_size, pair_rows)
    query_grad = (
        logit_scale
        * lax.dot_general(
            weights_t, items_all, (((0,), (0,)), ((), ())), preferred_element_type=jnp.float32
        )
    ).astype(jnp.bfloat16)
    item_sum = lax.psum_scatter(
        (logit_scale * jnp.dot(weights_t, query_out, preferred_element_type=jnp.float32)).astype(
            jnp.bfloat16
        ),
        "dp",
        scatter_dimension=0,
        tiled=True,
    )
    contract_last = (((1,), (1,)), ((), ()))
    query_pooled = lax.dot_general(
        query_grad, w_query, contract_last, preferred_element_type=jnp.float32
    ).astype(jnp.bfloat16)
    item_pooled = lax.dot_general(
        item_sum, w_item, contract_last, preferred_element_type=jnp.float32
    ).astype(jnp.bfloat16)
    contract_first = (((0,), (0,)), ((), ()))
    local_query_w = lax.dot_general(
        pooled_query, query_grad, contract_first, preferred_element_type=jnp.float32
    )
    local_item_w = lax.dot_general(
        pooled_item, item_sum, contract_first, preferred_element_type=jnp.float32
    )
    grad_w_query, grad_w_item = lax.psum((local_query_w, local_item_w), ("dp", "table"))
    owners = slot_owner[:, :, 0]
    local_rows = slot_row[:, :, 0]
    slots_pair = owners.shape[1]
    bag_size = slots_pair // 2
    emb_width = query_pooled.shape[1]
    table_count = lax.axis_size("table")
    slot_values = jnp.concatenate(
        [
            jnp.broadcast_to(query_pooled[:, None, :], (pair_rows, bag_size, emb_width)),
            jnp.broadcast_to(item_pooled[:, None, :], (pair_rows, bag_size, emb_width)),
        ],
        axis=1,
    ).reshape(-1, emb_width)
    flat_owner = owners.reshape(-1)
    flat_local = local_rows.reshape(-1)
    capacity = 2 * flat_owner.shape[0] // table_count
    owner_onehot = (
        flat_owner[:, None] == jnp.arange(table_count, dtype=jnp.int32)[None, :]
    ).astype(jnp.int32)
    slot_rank = jnp.sum(jnp.cumsum(owner_onehot, axis=0) * owner_onehot, axis=1) - 1
    send_values = (
        jnp.zeros((table_count, capacity, emb_width), jnp.bfloat16)
        .at[flat_owner, slot_rank]
        .set(slot_values)
    )
    send_rows = (
        jnp.zeros((table_count, capacity), jnp.int32).at[flat_owner, slot_rank].set(flat_local)
    )
    got_values, got_rows = (
        lax.all_to_all(send_values, "table", split_axis=0, concat_axis=0, tiled=True),
        lax.all_to_all(send_rows, "table", split_axis=0, concat_axis=0, tiled=True),
    )
    local_grad = (
        jnp.zeros((R_DEV, emb_width), jnp.float32)
        .at[got_rows.reshape(-1)]
        .add(got_values.reshape(-1, emb_width).astype(jnp.float32))
    )
    grad_table = lax.psum(local_grad.astype(jnp.bfloat16), "dp").astype(jnp.float32)
    return (grad_table, grad_w_query, grad_w_item)


def solution(mesh):
    placed = (
        P(("dp", "table"), None),
        P(("dp", "table"), None),
        P(("dp", "table"), None),
        P(("dp", "table"), None),
        P(),
        P(),
        P(("dp", "table")),
        P(("dp", "table"), None, None),
        P(("dp", "table"), None, None),
    )
    return jax.shard_map(
        on_device,
        mesh=mesh,
        in_specs=placed,
        out_specs=(P("table", None), P(), P()),
        check_vma=False,
    )
```

profile of v0, /device:TPU:8, one launch (start us, length us, event | category | flops | bytes accessed | tf_op | source)
XLA Modules:
  0.0 798.3 jit_solution(7120487123951979231)
XLA Ops:
  7.2 0.7 all-gather.2.cloned.1.call-update
  8.0 91.8 %all-gather.2.cloned.1.call-done = bf16[4096,256]{1,0:T(8,128)(2,1)} async-done(((bf16[128,256]{1,0:T(8,128)(2,1)}), bf16[4096,256]{1,0:T(8,128)(2,1)}) %all-gather.2.cloned.1.call-update) | async-done | bytes 2097168 | tf_op jit(solution)/shard_map/all_gather | solution.py:25
  99.8 6.4 while.25
  99.8 1.4 fusion.57
  101.2 0.2 exponential_reduce_fusion.2
  101.4 1.4 fusion.57
  102.8 0.2 exponential_reduce_fusion.2
  103.0 1.4 fusion.57
  104.4 0.2 exponential_reduce_fusion.2
  104.6 1.4 fusion.57
  106.0 0.2 exponential_reduce_fusion.2
  106.2 10.8 %while.24 = (s32[]{:T(128)}, bf16[4,1024,128]{2,1,0:T(8,128)(2,1)S(1)}, f32[128]{0:T(128)S(1)}, bf16[4,1024,256]{2,1,0:T(8,128)(2,1)}, bf16[128,256]{1,0:T(8,128...) while((s32[]{:T(128)}, ...), condition=%wide.region_9.10_spmd.clone, body=%wide.region_8.9_spmd.clone.sunk | while | flops 68158592 | bytes 863865 | solution.py:58
  106.2 0.6 dynamic_slice.28
  106.8 0.6 iota_add_fusion.5
  107.4 1.4 fusion.55
  108.9 0.6 dynamic_slice.28
  109.5 0.6 iota_add_fusion.5
  110.1 1.4 fusion.55
  111.6 0.6 dynamic_slice.28
  112.2 0.6 iota_add_fusion.5
  112.8 1.4 fusion.55
  114.3 0.6 dynamic_slice.28
  114.9 0.6 iota_add_fusion.5
  115.6 1.4 fusion.55
  117.0 2.9 fusion.19
  120.3 4.5 reduce-window.6
  124.9 0.4 slice_reduce_fusion
  125.3 0.2 reduce-window.9
  125.7 0.1 broadcast_add_fusion
  126.0 0.1 and_reduce_fusion
  126.1 8.6 %scatter_custom_fusion.1 = s32[4096]{0:T(1024)} fusion(s32[2048]{0:T(1024)S(1)} %broadcast_select_fusion.2, s32[2048]{0:T(1024)S(1)} %reshape.153, s32[]{:T(128)} %constant.12.clone.1), kind=kCustom, calls=%fused_computation.56 | custom fusion | bytes 16388
  134.7 7.3 all-to-all-start
  142.0 0.6 fusion.22
  142.6 0.2 convolution_convert_fusion.1
  142.8 196.5 %reduce-scatter.2.cloned.1.call-done = bf16[128,256]{1,0:T(8,128)(2,1)} async-done(((bf16[4096,256]{1,0:T(8,128)(2,1)}), bf16[128,256]{1,0:T(8,128)(2,1)}) %reduce-scatter.2.cloned.1.call-update) | async-done | bytes 65552 | tf_op jit(solution)/shard_map/reduce_scatter | solution.py:65
  339.3 1.0 convolution_convert_fusion
  340.5 6.8 scatter_custom_fusion.2
  347.3 7.4 all-to-all-start.1
  354.8 0.9 convolution_bitcast_fusion.1
  355.7 0.8 convolution_bitcast_fusion
  356.6 23.0 %all-to-all-done.1 = bf16[16,256,128]{2,1,0:T(8,128)(2,1)S(1)} async-done(((bf16[16,256,128]{2,1,0:T(8,128)(2,1)}), bf16[16,256,128]{2,1,0:T(8,128)(2,1)S(1)}, u32[]{:S(2)}, u32[]{:S(2)}) %all-to-all-start.1) | async-done | bytes 1048608 | tf_op jit(solution)/shard_map/all_to_all | solution.py:117
  379.6 22.9 %scatter_custom_fusion = f32[4096,128]{1,0:T(8,128)S(1)} fusion(s32[4096]{0:T(1024)S(1)} %bitcast.87, bf16[4096,128]{1,0:T(8,128)(2,1)S(1)} %bitcast.80, f32[]{:T(128)} %constant.33.clone.1), kind=kCustom, calls=%fused_computation.30 | custom fusion | flops 1048576 | bytes 3145732 | tf_op jit(solution)/shard_map/scatter-add | solution.py:123
  402.5 1.1 convert_element_type.42
  403.6 224.1 %all-reduce.6.cloned.1.call-done = (f32[128,256]{0,1:T(8,128)}, f32[128,256]{0,1:T(8,128)}) async-done(((f32[128,256]{0,1:T(8,128)}, f32[128,256]{0,1:T(8,128)}), (f32[128,256]{0,1:T(8,128)}, f32[128,256]{0,1:T(8,128)})) %all-reduce.6.cloned.1.call-update) | async-done | bytes 262160 | tf_op jit(solution)/shard_map/psum | solution.py:87
  627.7 1.7 copy.18
  629.4 1.7 copy.19
  631.0 158.1 %all-reduce.4.cloned.1.call-done = bf16[4096,128]{1,0:T(8,128)(2,1)} async-done(((bf16[4096,128]{1,0:T(8,128)(2,1)}), bf16[4096,128]{1,0:T(8,128)(2,1)}) %all-reduce.4.cloned.1.call-update) | async-done | bytes 1048592 | tf_op jit(solution)/shard_map/psum | solution.py:125
  789.1 2.7 convert_element_type.43
  (66 shorter events, 1.3 us)
Async XLA Ops:
  7.2 135.4 %copy-start = (bf16[128,256]{1,0:T(8,128)(2,1)S(1)}, bf16[128,256]{1,0:T(8,128)(2,1)}, u32[]{:S(2)}) copy-start(bf16[128,256]{1,0:T(8,128)(2,1)} %param.17) | copy-start | bytes 196612
  7.2 92.6 %all-gather.2.cloned.1.call-start = ((), (), s32[]{:S(2)}) async-start(), calls=%async_computation.3 | async-start | bytes 2162688 | tf_op jit(solution)/shard_map/all_gather | solution.py:25
  7.9 331.4 %reduce-scatter.2.cloned.1.call-start = ((), (), s32[]{:S(2)}) async-start(), calls=%async_computation.4 | async-start | bytes 2162688 | tf_op jit(solution)/shard_map/reduce_scatter | solution.py:65
  99.8 6.4 copy-start.10
  117.0 2.9 copy-start.6
  119.9 5.6 copy-start.7
  119.9 6.0 copy-start.9
  119.9 6.1 copy-start.8
  119.9 22.1 %copy-start.1 = (bf16[4,1024,256]{2,1,0:T(8,128)(2,1)S(1)}, bf16[4,1024,256]{2,1,0:T(8,128)(2,1)}, u32[]{:S(2)}) copy-start(bf16[4,1024,256]{2,1,0:T(8,128)(2,1)} %get-tuple-element.312) | copy-start | bytes 6291460
  125.3 214.0 %copy-start.3 = (bf16[128,256]{1,0:T(8,128)(2,1)S(1)}, bf16[128,256]{1,0:T(8,128)(2,1)}, u32[]{:S(2)}) copy-start(bf16[128,256]{1,0:T(8,128)(2,1)} %param.18) | copy-start | bytes 196612
  134.7 212.6 %all-to-all-start = ((s32[16,1,256]{2,1,0:T(1,128)}), s32[16,1,256]{2,1,0:T(1,128)S(1)}, u32[]{:S(2)}, u32[]{:S(2)}) async-start(s32[16,1,256]{2,1,0:T(1,128)} %bitcast.3), calls=%async_computation | async-start | bytes 32768 | tf_op jit(solution)/shard_map/all_to_all | solution.py:118
  340.4 14.4 %copy-start.4 = (bf16[128,128]{1,0:T(8,128)(2,1)S(1)}, bf16[128,128]{1,0:T(8,128)(2,1)}, u32[]{:S(2)}) copy-start(bf16[128,128]{1,0:T(8,128)(2,1)} %param.15) | copy-start | bytes 98308
  340.4 15.2 %copy-start.2 = (bf16[128,256]{1,0:T(8,128)(2,1)S(1)}, bf16[128,256]{1,0:T(8,128)(2,1)}, u32[]{:S(2)}) copy-start(bf16[128,256]{1,0:T(8,128)(2,1)} %reduce-scatter.2.cloned.1.call-done) | copy-start | bytes 196612
  340.4 15.2 %copy-start.5 = (bf16[128,128]{1,0:T(8,128)(2,1)S(1)}, bf16[128,128]{1,0:T(8,128)(2,1)}, u32[]{:S(2)}) copy-start(bf16[128,128]{1,0:T(8,128)(2,1)} %param.16) | copy-start | bytes 98308
  347.3 32.2 %all-to-all-start.1 = ((bf16[16,256,128]{2,1,0:T(8,128)(2,1)}), bf16[16,256,128]{2,1,0:T(8,128)(2,1)S(1)}, u32[]{:S(2)}, u32[]{:S(2)}) async-start(bf16[16,256,128]{2,1,0:T(8,128)(2,1)} %bitcast.9), calls=%async_computation.2 | async-start | bytes 2097152 | tf_op jit(solution)/shard_map/all_to_all | solution.py:117
  354.7 272.9 %all-reduce.6.cloned.1.call-start = ((), (), s32[]{:S(2)}) async-start(), calls=%async_computation.6 | async-start | bytes 524288 | tf_op jit(solution)/shard_map/psum | solution.py:87
  356.5 432.5 %all-reduce.4.cloned.1.call-start = ((), (), s32[]{:S(2)}) async-start(), calls=%async_computation.5 | async-start | bytes 2097152 | tf_op jit(solution)/shard_map/psum | solution.py:125
Sparse Core Ops, SparseCore 0:
  11.2 88.5 all-gather.1
  120.0 219.2 reduce-scatter.1
  362.2 265.4 all-reduce.5
  631.6 157.4 all-reduce.3
where the time goes:
time: 799 us; the launch traced here: 798 us
  waiting for transfers between devices  694 us (87%)
  other arithmetic  35.2 us (4%)
  local copies, waits for them, and re-layouts  22.2 us (3%)
  matrix products  17.6 us (2%)
  starting transfers between devices  14.8 us (2%)
  between operations  14 us (2%)
    psum x1, waiting for transfers between devices, on_device(): lax.psum((local_query_w, local_item_w), ('dp', 'table'))  224 us
    reduce_scatter x1, waiting for transfers between devices, on_device(): lax.psum_scatter((logit_scale * jnp.dot(weights_t, query_out, preferred_e...  197 us
    psum x1, waiting for transfers between devices, on_device(): lax.psum(local_grad.astype(jnp.bfloat16), 'dp').astype(jnp.float32)  158 us
    all_gather x1, waiting for transfers between devices, on_device(): items_all = lax.all_gather(item_out, 'dp', axis=0, tiled=True)  91.8 us
    all_to_all x1, waiting for transfers between devices, on_device(): lax.all_to_all(send_values, 'table', split_axis=0, concat_axis=0, tiled=T...  23 us
    scatter-add x1, other arithmetic, on_device(): local_grad = jnp.zeros((R_DEV, emb_width), jnp.float32).at[got_rows.resha...  22.9 us
    unnamed x28, local copies, waits for them, and re-layouts  19 us
  transfers between devices with their start and end apart: 6, of which 5 were waited for; matrix products, arithmetic and copies ran while one was open for 7% of the time, Pallas kernels for 0%

commit v1 on v0

v1 whole, which is shorter than its diff:
```python
import math

import jax
import jax.numpy as jnp
from jax import lax
from jax.experimental import pallas as pl
from jax.experimental.pallas import tpu as pltpu
from jax.sharding import PartitionSpec as P

MESH = pl.DeviceIdType.MESH
F32, BF16, I32 = jnp.float32, jnp.bfloat16, jnp.int32
NX, NZ, NY = 4, 8, 8
B, W, E = 128, 256, 128
NT = 2 * NY
CAP = 256
SCALE = 1.0 / math.sqrt(W)
N_COPIES = 176

NN = (((1,), (0,)), ((), ()))
NT_DIMS = (((1,), (1,)), ((), ()))
TN = (((0,), (0,)), ((), ()))


def dot(a, b, dims=NN):
    return lax.dot_general(a, b, dims, preferred_element_type=F32)


def iota(shape, dim):
    return lax.broadcasted_iota(I32, shape, dim)


ARRIVE = (0, 2, 6, 1, 7, 3, 5, 4)
POS = {d: p for p, d in enumerate(ARRIVE)}
OWN = (0, 1, 2, 3, 4, 10, 11, 12)
SIB = (5, 6, 7, 8, 9, 13, 14, 15)
FIRST = 10 * CAP


def kernel(
    q_ref, it_ref, pq_ref, pi_ref, wq_ref, wi_ref, pw_ref, ow_ref, rw_ref,
    table_ref, gw_ref,
    pq, pi, wq, wi, pw, ow, rw,
    ibuf, qbuf, ebuf, gbuf, tops, totals, st_send, st_recv,
    gi_send, gi_relay, gi_half, gi_recv, gi_own, gq_send, gq_recv, gq_own,
    taken, slots_a, slots_b, list_send, list_recv, lists, low_row, onehot, select, factor, pooled, values,
    w_part, wx_recv, wz_send, wz_recv, wy_recv,
    t_own, t_send, tx_half, tx_relay, tx_recv, tz_own, tz_send, tz_recv, t_back,
    load_sem, send_sem, recv_sem,
):
    dp, tb = lax.axis_index("dp"), lax.axis_index("table")
    x, z = lax.div(dp, NZ), lax.rem(dp, NZ)
    y, core = lax.div(tb, 2), lax.rem(tb, 2)

    def at_x(d):
        return (lax.rem(x + d + NX, NX) * NZ + z, tb)

    def at_z(d):
        return (x * NZ + lax.rem(z + d + NZ, NZ), tb)

    def at_y(d):
        return (dp, lax.rem(y + d + NY, NY) * 2 + core)

    sibling = (dp, tb + 1 - 2 * core)
    partners = (
        [at_x(d) for d in range(1, NX)]
        + [at_z(d) for d in range(1, NZ)]
        + [at_y(d) for d in range(1, NY)]
        + [sibling]
    )
    barrier = pltpu.get_barrier_semaphore()
    for partner in partners:
        pl.semaphore_signal(barrier, inc=1, device_id=partner, device_id_type=MESH)
    loads = [
        pltpu.make_async_copy(src, dst, load_sem.at[i])
        for i, (src, dst) in enumerate((
            (it_ref, ibuf.at[pl.ds(0, B), :]),
            (q_ref, qbuf.at[pl.ds(0, B), :]),
            (ow_ref, ow),
            (rw_ref, rw),
            (pw_ref, pw),
            (pq_ref, pq),
            (pi_ref, pi),
            (wq_ref, wq),
            (wi_ref, wi),
        ))
    ]
    for load in loads:
        load.start()
    pl.semaphore_wait(barrier, len(partners))

    copies, drained = [], [0]

    def remote(index, src, dst, device):
        return pltpu.make_async_remote_copy(
            src_ref=src,
            dst_ref=dst,
            send_sem=send_sem.at[index],
            recv_sem=recv_sem.at[index],
            device_id=device,
            device_id_type=MESH,
        )

    def send(src, dst, device):
        copy = remote(len(copies), src, dst, device)
        copy.start()
        copies.append(copy)
        return copy

    def drain():
        for copy in copies[drained[0]:]:
            copy.wait_send()
        drained[0] = len(copies)

    def gather_start(slot, at, source=None):
        source = slot(0, None) if source is None else source
        return {d: send(source, slot(d % 8, None), at(d)) for d in (2, -2, 1, -1)}

    def gather_pass(got, slot, at):
        got[2].wait_recv()
        got[3] = send(slot(2, None), slot(3, None), at(1))
        got[4] = send(slot(2, 0), slot(4, 0), at(2))
        got[-2].wait_recv()
        got[-3] = send(slot(6, None), slot(5, None), at(-1))
        got[-4] = send(slot(6, 1), slot(4, 1), at(-2))

    def wait_for(got, *names):
        for name in names:
            got[name].wait_recv()

    def item_slot(d, half):
        if half is None:
            return ibuf.at[pl.ds(POS[d] * B, B), :]
        return ibuf.at[pl.ds(POS[d] * B + half * 64, 64), :]

    item_in = gather_start(item_slot, at_z, it_ref)
    query_in = {}
    for d in (1, 3, 2):
        query_in[d] = send(q_ref, qbuf.at[pl.ds(d * B, B), :], at_x(d))

    for load in loads:
        load.wait()
    owner_row = iota((NT, B), 0)
    hits = jnp.concatenate([(ow[k:k + 1, :] == owner_row).astype(F32) for k in range(16)], axis=0)
    before = (iota((B, 2 * B), 0) < iota((B, 2 * B), 1)).astype(BF16)
    counts = dot(hits.astype(BF16), before)
    at_row, at_col = iota((256, 256), 0), iota((256, 256), 1)
    earlier = jnp.logical_and(
        lax.bitwise_and(at_row, 15) == lax.bitwise_and(at_col, 15),
        lax.shift_right_logical(at_col, 4) < lax.shift_right_logical(at_row, 4),
    ).astype(BF16)
    taken[...] = (counts[:, 0:B] + dot(earlier, counts[:, B:].astype(BF16))) * hits
    list_row = iota((B, B), 0)
    list_owner, piece = lax.shift_right_logical(list_row, 3), lax.bitwise_and(list_row, 7)
    pair = iota((1, B), 1)
    place = iota((CAP, B), 0)

    def list_slot(k, _):
        lanes = pl.ds(pl.multiple_of(k * B, B), B)
        ranks = taken[pl.ds(pl.multiple_of(k * NT, NT), NT), :]
        rank = jnp.sum(ranks, axis=0, keepdims=True).astype(I32)
        slots_b[:, lanes] = (place == rank).astype(BF16)
        owner, row = ow[pl.ds(k, 1), :], rw[pl.ds(k, 1), :]
        part = jnp.where(
            piece == 0,
            pair + lax.div(k, 8) * B,
            jnp.where(
                piece == 1,
                lax.shift_right_logical(row, 8) + 1,
                jnp.where(piece == 2, lax.bitwise_and(row, 255), 0),
            ),
        )
        slots_a[:, lanes] = jnp.where(list_owner == owner, part, 0).astype(F32).astype(BF16)
        return 0

    lax.fori_loop(0, 16, list_slot, 0)
    list_send[...] = dot(slots_a[...], slots_b[...], NT_DIMS)
    list_in = {}
    for d in ARRIVE[1:]:
        to_y = lax.rem(y + d, NY)
        list_in[d] = send(
            list_send.at[pl.ds(pl.multiple_of(to_y * 16, 16), 16), :], list_recv.at[POS[d]], at_y(d)
        )
    list_recv[0] = list_send[pl.ds(pl.multiple_of(y * 16, 16), 16), :]

    gather_pass(item_in, item_slot, at_z)

    wait_for(query_in, 1, 3, 2)

    def logits(p, _):
        rows = pl.ds(pl.multiple_of(p * B, B), B)
        block = SCALE * dot(ibuf[rows, :], qbuf[...], NT_DIMS)
        top = jnp.max(block, axis=0, keepdims=True)
        block = jnp.exp(block - top)
        ebuf[rows, :] = block
        tops[pl.ds(p, 1), :] = top
        totals[pl.ds(p, 1), :] = jnp.sum(block, axis=0, keepdims=True)
        return 0

    wait_for(item_in, 1, -1)
    lax.fori_loop(0, 5, logits, 0)

    mine = pl.ds(pl.multiple_of(core * 8, 8), 8)
    other = pl.ds(pl.multiple_of((1 - core) * 8, 8), 8)
    for d in ARRIVE[1:]:
        list_in[d].wait_recv()
    list_sib = []
    for low, high in ((0, 5), (5, 8)):
        list_sib.append(send(
            list_recv.at[pl.ds(low, high - low), other, :],
            lists.at[pl.ds(SIB[low], high - low)],
            sibling,
        ))
        for p in range(low, high):
            lists[OWN[p]] = list_recv[p, mine, :]

    source_row = iota((2 * B, CAP), 0)
    low_row[...] = lax.bitwise_and(iota((1152, B), 0), 1023).astype(jnp.int16)

    def one_hots(s, _):
        entry = lists[s]
        row = (entry[1:2, :].astype(I32) - 1) * 256 + entry[2:3, :].astype(I32)
        select[s] = (entry[0:1, :].astype(I32) == source_row).astype(BF16)
        low = jnp.broadcast_to(lax.bitwise_and(row, 1023), (16, CAP)).astype(jnp.int16)
        for side in (0, 1):
            lanes = pl.ds(pl.multiple_of(s * CAP + side * B, B), B)
            same = low_row[...] == jnp.tile(low[:, side * B:(side + 1) * B], (72, 1))
            onehot[:, lanes] = jnp.where(same, jnp.ones((), BF16), jnp.zeros((), BF16))
        block = jnp.broadcast_to(lax.shift_right_arithmetic(row, 10), (16, CAP))
        for j in range(NX):
            factor[s, j] = (block == j).astype(BF16)
        return 0

    own_first, own_last = (0, 5), (10, 13)
    lax.fori_loop(*own_first, one_hots, 0)
    wait_for(item_in, 3, -3)
    lax.fori_loop(5, 7, logits, 0)
    lax.fori_loop(*own_last, one_hots, 0)
    wait_for(item_in, 4, -4)
    lax.fori_loop(7, 8, logits, 0)

    top = jnp.max(tops[...], axis=0, keepdims=True)
    total = jnp.sum(totals[...] * jnp.exp(tops[...] - top), axis=0, keepdims=True)
    weight = pw[...]
    for k in range(NX):
        st_send[k:k + 1, :] = top[:, k * B:(k + 1) * B]
        st_send[NX + k:NX + k + 1, :] = total[:, k * B:(k + 1) * B]
    st_send[8:16, :] = jnp.broadcast_to(weight, (8, B))
    stat_in = {d: send(st_send, st_recv.at[d], at_x(d)) for d in (2, 1, 3)}
    for copy in list_sib:
        copy.wait_recv()
    lax.fori_loop(5, 10, one_hots, 0)
    lax.fori_loop(13, 16, one_hots, 0)
    wait_for(stat_in, 1, 3, 2)
    maxima, factors = [], []
    for k in range(NX):
        part_tops, part_totals = [st_send[k:k + 1, :]], [st_send[NX + k:NX + k + 1, :]]
        for d in range(1, NX):
            j = (k - d) % NX
            part_tops.append(st_recv[d, j:j + 1, :])
            part_totals.append(st_recv[d, NX + j:NX + j + 1, :])
        row_max = part_tops[0]
        for t in part_tops[1:]:
            row_max = jnp.maximum(row_max, t)
        row_total = sum(s * jnp.exp(t - row_max) for t, s in zip(part_tops, part_totals))
        maxima.append(row_max)
        factors.append((weight if k == 0 else st_recv[k, 8:9, :]) / row_total)
    row_max, factors = jnp.concatenate(maxima, axis=1), jnp.concatenate(factors, axis=1)
    totals[...] = factors * jnp.exp(tops[...] - row_max)

    def item_terms(p):
        rows = pl.ds(pl.multiple_of(p * B, B), B)
        block = (ebuf[rows, :] * totals[pl.ds(p, 1), :]).astype(BF16)
        gbuf[rows, :] = block
        return SCALE * dot(block, qbuf[...])

    def far_terms(p, _):
        gi_send[p] = item_terms(p).astype(BF16)
        return 0

    def near_terms(p, _):
        gi_own[p] = item_terms(p)
        return 0

    lax.fori_loop(7, 8, far_terms, 0)
    half_in = [
        send(gi_send.at[7, pl.ds(0, 64), :], gi_half.at[0], at_z(2)),
        send(gi_send.at[7, pl.ds(64, 64), :], gi_half.at[1], at_z(-2)),
    ]
    lax.fori_loop(5, 7, far_terms, 0)
    relay_in = [
        send(gi_send.at[POS[5]], gi_relay.at[0], at_z(1)),
        send(gi_send.at[POS[3]], gi_relay.at[1], at_z(-1)),
    ]
    lax.fori_loop(3, 5, far_terms, 0)
    grad_in = {d: send(gi_send.at[POS[d]], gi_recv.at[POS[d]], at_z(-d)) for d in (7, 1)}
    lax.fori_loop(0, 3, near_terms, 0)
    same = iota((B, B), 0) == iota((B, B), 1)
    diagonal = ebuf[0:B, 0:B] * totals[0:1, 0:B] - jnp.where(same, weight, 0.0)
    gbuf[0:B, 0:B] = diagonal.astype(BF16)
    gi_own[0] = SCALE * dot(gbuf[0:B, :], qbuf[...])

    terms = SCALE * dot(gbuf[...], ibuf[...], TN)
    gq_own[...] = terms[0:B, :]
    for k in range(1, NX):
        gq_send[k] = terms[k * B:(k + 1) * B, :].astype(BF16)
    query_grad_in = {k: send(gq_send.at[k], gq_recv.at[k], at_x(-k)) for k in (2, 1, 3)}
    for side, (d, rows) in enumerate(((6, slice(0, 64)), (2, slice(64, 128)))):
        p = POS[d]
        relay_in[side].wait_recv()
        half_in[side].wait_recv()
        gi_own[p] += gi_relay[side].astype(F32)
        gi_own[p, rows, :] += gi_half[side].astype(F32)
        gi_send[p] = gi_own[p].astype(BF16)
        grad_in[d] = send(gi_send.at[p], gi_recv.at[p], at_z(-d))

    query_grad = gq_own[...]
    for k in (1, 3, 2):
        query_grad_in[k].wait_recv()
        query_grad += gq_recv[k].astype(F32)
    query_grad = query_grad.astype(BF16)

    pooled_in, pooled_sib = {}, {}

    def pooled_slot(half):
        def slot(d, rows):
            rows = pl.ds(0, E) if rows is None else pl.ds(rows * 64, 64)
            return pooled.at[OWN[POS[d]], rows, pl.ds(half * B, B)]

        return slot

    def to_sibling(half, low, high):
        lanes = pl.ds(half * B, B)
        pooled_sib[half, low] = send(
            pooled.at[pl.ds(OWN[low], high - low), :, lanes],
            pooled.at[pl.ds(SIB[low], high - low), :, lanes],
            sibling,
        )

    pooled[0, :, 0:B] = dot(wq[...], query_grad, NT_DIMS).astype(BF16)
    pooled_in[0] = gather_start(pooled_slot(0), at_y)
    to_sibling(0, 0, 1)
    w_part[0:B, :] = dot(pq[...], query_grad, TN)

    gather_pass(pooled_in[0], pooled_slot(0), at_y)
    wait_for(pooled_in[0], 1, -1)
    to_sibling(0, 1, 3)
    to_sibling(0, 3, 5)
    drain()

    item_grad = gi_own[0]
    for d in (1, 7, 2, 6):
        grad_in[d].wait_recv()
        item_grad += gi_recv[POS[d]].astype(F32)
    item_grad = item_grad.astype(BF16)
    pooled[0, :, B:] = dot(wi[...], item_grad, NT_DIMS).astype(BF16)
    pooled_in[1] = gather_start(pooled_slot(1), at_y)
    to_sibling(1, 0, 1)
    w_part[B:, :] = dot(pi[...], item_grad, TN)
    w_in = {}
    for d in (2, 1, 3):
        to_x = lax.rem(x + d, NX)
        w_in[d] = send(w_part.at[pl.ds(pl.multiple_of(to_x * 64, 64), 64), :], wx_recv.at[d], at_x(d))
    wait_for(pooled_in[0], 3, -3, 4, -4)
    to_sibling(0, 5, 8)

    def place_values(s, _):
        got = dot(pooled[s], select[s]).astype(BF16)
        lanes = pl.ds(pl.multiple_of(s * CAP, CAP), CAP)
        for j in range(NX):
            values[j * E:(j + 1) * E, lanes] = got * jnp.tile(factor[s, j], (8, 1))
        return 0

    def quarter_rows(p):
        return pl.ds(pl.multiple_of(lax.rem(z + 4 + p * (p + 1), NZ) * B, B), 256)

    def first_part(p, _):
        t_own[p] = dot(values[:, 0:FIRST], onehot[quarter_rows(p), 0:FIRST], NT_DIMS)
        return 0

    gather_pass(pooled_in[1], pooled_slot(1), at_y)
    wait_for(pooled_in[1], 1, -1)
    to_sibling(1, 1, 3)
    to_sibling(1, 3, 5)
    lax.fori_loop(0, 5, place_values, 0)
    for low in (0, 1, 3):
        pooled_sib[0, low].wait_recv()
        pooled_sib[1, low].wait_recv()
    lax.fori_loop(5, 10, place_values, 0)
    wait_for(pooled_in[1], 3, -3, 4, -4)
    to_sibling(1, 5, 8)
    lax.fori_loop(0, 2, first_part, 0)
    pooled_sib[0, 5].wait_recv()
    pooled_sib[1, 5].wait_recv()
    lax.fori_loop(10, 16, place_values, 0)

    half_base = len(copies)
    copies.extend([None] * 8)

    def half_copy(p, side):
        far = lax.rem(x + 2, NX)
        rows = pl.ds(pl.multiple_of(far * E + side * 64, 64), 64)
        return remote(
            half_base + 2 * p + side, t_send.at[p, rows, :], tx_half.at[p, side], at_x(1 - 2 * side)
        )

    def send_part(p, part):
        t_own[p] = part
        t_send[p] = part.astype(BF16)
        half_copy(p, 0).start()
        half_copy(p, 1).start()

    def last_part(p, _):
        send_part(p, t_own[p] + dot(values[:, FIRST:], onehot[quarter_rows(p), FIRST:], NT_DIMS))
        return 0

    def whole_part(p, _):
        send_part(p, dot(values[...], onehot[quarter_rows(p), :], NT_DIMS))
        return 0

    lax.fori_loop(0, 2, last_part, 0)
    lax.fori_loop(2, 3, whole_part, 0)
    for p in range(4):
        for side in (0, 1):
            copies[half_base + 2 * p + side] = half_copy(p, side)

    relay_in, tz_in = {}, {}

    def table_relay(p):
        for side, step in ((0, 1), (1, -1)):
            copies[half_base + 2 * p + side].wait_recv()
            near = lax.rem(x + step + NX, NX) * E
            for half in (0, 1):
                rows = slice(half * 64, half * 64 + 64)
                part = t_own[p, pl.ds(pl.multiple_of(near + half * 64, 64), 64), :]
                if half == side:
                    part += tx_half[p, side].astype(F32)
                tx_relay[p, side, rows, :] = part.astype(BF16)
            relay_in[p, side] = send(tx_relay.at[p, side], tx_recv.at[p, side], at_x(step))

    def table_sum(p):
        part = t_own[p, pl.ds(pl.multiple_of(x * E, E), E), :]
        for side in (0, 1):
            relay_in[p, side].wait_recv()
            part += tx_recv[p, side].astype(F32)
        for side in (0, 1):
            d = (4 + p * (p + 1)) % NZ + side
            if d == 0:
                tz_own[...] = part[:, 0:B]
            else:
                tz_send[d] = part[:, side * B:(side + 1) * B].astype(BF16)
                tz_in[d] = send(tz_send.at[d], tz_recv.at[d], at_z(d))

    table_relay(0)
    table_relay(1)
    lax.fori_loop(3, 4, whole_part, 0)
    table_sum(0)
    table_relay(2)
    table_sum(1)

    w_sum = w_part[pl.ds(pl.multiple_of(x * 64, 64), 64), :]
    for d in (1, 3, 2):
        w_in[d].wait_recv()
        w_sum += wx_recv[d]
    wz_send[...] = w_sum
    wz_in = {}
    for d in ARRIVE[1:]:
        to_z = lax.rem(z + d, NZ)
        wz_in[d] = send(wz_send.at[pl.ds(pl.multiple_of(to_z * 8, 8), 8), :], wz_recv.at[d], at_z(d))

    table_relay(3)

    w_sum = wz_send[pl.ds(pl.multiple_of(z * 8, 8), 8), :]
    for d in ARRIVE[1:]:
        wz_in[d].wait_recv()
        w_sum += wz_recv[d]
    wy_recv[0, 0] = w_sum
    wy_in = {d: send(wy_recv.at[0, 0], wy_recv.at[0, d], at_y(d)) for d in ARRIVE[1:]}

    table_sum(2)
    drain()
    table_sum(3)

    part = tz_own[...]
    for d in (4, 5, 6, 7, 2, 3, 1):
        tz_in[d].wait_recv()
        part += tz_recv[d].astype(F32)
    t_back[x, 0] = part.T.astype(BF16)

    def back_slot(d, half):
        if half is None:
            return t_back.at[x, POS[d]]
        return t_back.at[x, POS[d], pl.ds(half * 64, 64), :]

    back = gather_start(back_slot, at_z)
    near_in, far_in = {}, []

    def to_near(low, high):
        rows = t_back.at[x, pl.ds(low, high - low)]
        for side, step in ((0, 1), (1, -1)):
            near_in[low, side] = send(rows, rows, at_x(step))

    def to_far(low, high):
        middle = {1: None, 2: low + 1, 3: None}[high - low]
        for side, step in ((0, 1), (1, -1)):
            near_in[low, side].wait_recv()
            held = lax.rem(x - step + NX, NX)
            if middle is None:
                rows = t_back.at[held, pl.ds(low, high - low), pl.ds(side * 64, 64), :]
            else:
                rows = t_back.at[held, low + side]
            far_in.append(send(rows, rows, at_x(step)))

    to_near(0, 1)

    for d in ARRIVE[1:]:
        wy_in[d].wait_recv()
    wy_sib = send(wy_recv.at[0], wy_recv.at[1], sibling)
    gather_pass(back, back_slot, at_z)
    to_near(1, 3)
    to_far(0, 1)
    wait_for(back, 1, -1)
    to_near(3, 5)
    wy_sib.wait_recv()
    w_sum = wy_recv[0, 0]
    for d in range(1, NY):
        w_sum += wy_recv[0, d]
    for d in range(NY):
        w_sum += wy_recv[1, d]

    def w_rows(place):
        return gw_ref.at[pl.ds(pl.multiple_of(place * 8, 8), 8), :]

    gw_ref[pl.ds(pl.multiple_of(dp * 8, 8), 8), :] = w_sum
    w_back = {d: send(w_rows(dp), w_rows(dp), at_z(d)) for d in ARRIVE[1:]}
    to_far(1, 3)
    wait_for(back, 3, -3, 4, -4)
    to_near(5, 8)
    to_far(3, 5)

    def rows_of(far, p, d):
        place = far * NZ + lax.rem(z - d + NZ, NZ)
        table_ref[pl.ds(pl.multiple_of(place * B, B), B), :] = t_back[far, p]

    wait_for(w_back, *ARRIVE[1:])
    w_held = gw_ref.at[pl.ds(pl.multiple_of(x * 64, 64), 64), :]
    for step in (2, 1, 3):
        far_in.append(send(w_held, w_held, at_x(step)))
    to_far(5, 8)
    for p, d in enumerate(ARRIVE):
        rows_of(x, p, d)
        rows_of(lax.rem(x + 1, NX), p, d)
        rows_of(lax.rem(x + 3, NX), p, d)
    for copy in far_in:
        copy.wait_recv()
    for p, d in enumerate(ARRIVE):
        rows_of(lax.rem(x + 2, NX), p, d)
    drain()


def finish(table_ref, gw_ref, out_ref, gwq_ref, gwi_ref):
    out_ref[...] = table_ref[...].astype(F32)

    @pl.when(pl.program_id(0) == 0)
    def _():
        gwq_ref[...] = gw_ref[0:B, :]
        gwi_ref[...] = gw_ref[B:, :]


def on_device(q, it, pq, pi, wq, wi, pw, owner, row):
    def vmem(*shape, dtype=F32):
        return pltpu.VMEM(shape, dtype)

    table, gw = pl.pallas_call(
        kernel,
        out_shape=(
            jax.ShapeDtypeStruct((4096, E), BF16),
            jax.ShapeDtypeStruct((2 * B, W), F32),
        ),
        in_specs=[pl.BlockSpec(memory_space=pltpu.HBM)] * 9,
        out_specs=(pl.BlockSpec(memory_space=pltpu.VMEM),) * 2,
        scratch_shapes=[
            vmem(B, E, dtype=BF16),
            vmem(B, E, dtype=BF16),
            vmem(E, W, dtype=BF16),
            vmem(E, W, dtype=BF16),
            vmem(1, B),
            vmem(16, B, dtype=I32),
            vmem(16, B, dtype=I32),
            vmem(NZ * B, W, dtype=BF16),
            vmem(NX * B, W, dtype=BF16),
            vmem(NZ * B, NX * B),
            vmem(NZ * B, NX * B, dtype=BF16),
            vmem(NZ, NX * B),
            vmem(NZ, NX * B),
            vmem(16, B),
            vmem(NX, 16, B),
            vmem(NZ, B, W, dtype=BF16),
            vmem(2, B, W, dtype=BF16),
            vmem(2, 64, W, dtype=BF16),
            vmem(NZ, B, W, dtype=BF16),
            vmem(3, B, W),
            vmem(NX, B, W, dtype=BF16),
            vmem(NX, B, W, dtype=BF16),
            vmem(B, W),
            vmem(256, B),
            vmem(B, 16 * B, dtype=BF16),
            vmem(CAP, 16 * B, dtype=BF16),
            vmem(B, CAP),
            vmem(NY, 16, CAP),
            vmem(NT, 8, CAP),
            vmem(1152, B, dtype=jnp.int16),
            vmem(1152, NT * CAP, dtype=BF16),
            vmem(NT, 2 * B, CAP, dtype=BF16),
            vmem(NT, NX, 16, CAP, dtype=BF16),
            vmem(NT, E, 2 * B, dtype=BF16),
            vmem(NX * E, NT * CAP, dtype=BF16),
            vmem(2 * B, W),
            vmem(NX, 64, W),
            vmem(64, W),
            vmem(NZ, 8, W),
            vmem(2, NY, 8, W),
            vmem(4, NX * E, 256),
            vmem(4, NX * E, 256, dtype=BF16),
            vmem(4, 2, 64, 256, dtype=BF16),
            vmem(4, 2, E, 256, dtype=BF16),
            vmem(4, 2, E, 256, dtype=BF16),
            vmem(E, B),
            vmem(NZ, E, B, dtype=BF16),
            vmem(NZ, E, B, dtype=BF16),
            vmem(NX, NZ, B, E, dtype=BF16),
            pltpu.SemaphoreType.DMA((9,)),
            pltpu.SemaphoreType.DMA((N_COPIES,)),
            pltpu.SemaphoreType.DMA((N_COPIES,)),
        ],
        compiler_params=pltpu.CompilerParams(
            collective_id=0, has_side_effects=True, vmem_limit_bytes=40 * 1024 * 1024
        ),
    )(*[
        pltpu.with_memory_space_constraint(a, pltpu.HBM)
        for a in (
            q, it, pq, pi, wq, wi, pw.reshape(1, B), owner.reshape(B, 16).T, row.reshape(B, 16).T
        )
    ])
    whole_w = pl.BlockSpec((B, W), lambda i: (0, 0))
    return pl.pallas_call(
        finish,
        grid=(4,),
        out_shape=(
            jax.ShapeDtypeStruct((4096, E), F32),
            jax.ShapeDtypeStruct((B, W), F32),
            jax.ShapeDtypeStruct((B, W), F32),
        ),
        in_specs=[
            pl.BlockSpec((1024, E), lambda i: (i, 0)),
            pl.BlockSpec((2 * B, W), lambda i: (0, 0)),
        ],
        out_specs=(pl.BlockSpec((1024, E), lambda i: (i, 0)), whole_w, whole_w),
        compiler_params=pltpu.CompilerParams(vmem_limit_bytes=8 * 1024 * 1024),
    )(table, gw)


def solution(mesh):
    both = ("dp", "table")
    placed = (
        P(both, None),
        P(both, None),
        P(both, None),
        P(both, None),
        P(),
        P(),
        P(both),
        P(both, None, None),
        P(both, None, None),
    )
    return jax.shard_map(
        on_device,
        mesh=mesh,
        in_specs=placed,
        out_specs=(P("table", None), P(), P()),
        check_vma=False,
    )
```

time: 799 us -> 99.4 us (0.12)
  the two profiles are of different devices: /device:TPU:8 before, /device:TPU:2 now
where the time goes in v1:
time: 99.4 us; the launch traced here: 99.3 us
  Pallas kernels  98.6 us (99%)
    pallas_call x1, Pallas kernels, on_device(): pl.pallas_call(kernel, out_shape=(jax.ShapeDtypeStruct((4096, E), BF16),...  96.7 us

profile of v1, /device:TPU:2, one launch (start us, length us, event | category | flops | bytes accessed | tf_op | source)
XLA Modules:
  0.0 99.3 jit_solution(3267862308151114609)
XLA Ops:
  0.6 96.7 %shard_map.112 = (bf16[4096,128]{1,0:T(8,128)(2,1)S(1)}, f32[256,256]{1,0:T(8,128)S(1)}) custom-call(bf16[128,256]{1,0:T(8,128)(2,1)} %q_ref.1, bf16[128,256]{1,0:T(8,128)(2,1)} %it_ref.1, bf16[128,128]{1,0:T(8,128)(2,1)} %pq_ref.1, bf16[128,128]{1,0:T(8,128)(2,1)} %pi_ref.1, bf16[128,256]{1,0:T(8,128)(2,1)} %wq_ref.1, bf16[128,256]{1,0:T(8,128)(2,1)} %wi_ref.1, ...), custom_call_target="tpu_custom_call" | custom-call | tf_op jit(solution)/shard_map/pallas_call | solution.py:573
  97.3 2.0 %shard_map.113 = (f32[4096,128]{1,0:T(8,128)}, f32[128,256]{1,0:T(8,128)}, f32[128,256]{1,0:T(8,128)}) custom-call(bf16[4096,128]{1,0:T(8,128)(2,1)S(1)} %get-tuple-element.5.table_ref, f32[256,256]{1,0:T(8,128)S(1)} %get-tuple-element.6.gw_ref), custom_call_target="tpu_custom_call" | custom-call | tf_op jit(solution)/shard_map/pallas_call | solution.py:645

commit v2 on v1

--- a/solution.py
+++ b/solution.py
@@ -42,9 +42,10 @@
     pq, pi, wq, wi, pw, ow, rw,
     ibuf, qbuf, ebuf, gbuf, tops, totals, st_send, st_recv,
     gi_send, gi_relay, gi_half, gi_recv, gi_own, gq_send, gq_recv, gq_own,
-    taken, slots_a, slots_b, list_send, list_recv, lists, low_row, onehot, select, factor, pooled, values,
+    taken, slots_a, slots_b, list_send, list_recv, lists, onehot, select, factor, pooled, values,
     w_part, wx_recv, wz_send, wz_recv, wy_recv,
-    t_own, t_send, tx_half, tx_relay, tx_recv, tz_own, tz_send, tz_recv, t_back,
+    t_own, t_send, tx_half, tx_relay, tx_recv, tz_first, tz_own, tz_send, tz_half, tz_relay, tz_back, tz_recv,
+    lz_half, lz_relay, lz_own, lz_send, lz_recv, lx_send, lx_recv, t_back, l_back,
     load_sem, send_sem, recv_sem,
 ):
     dp, tb = lax.axis_index("dp"), lax.axis_index("table")
@@ -199,42 +200,8 @@
     wait_for(item_in, 1, -1)
     lax.fori_loop(0, 5, logits, 0)
 
-    mine = pl.ds(pl.multiple_of(core * 8, 8), 8)
-    other = pl.ds(pl.multiple_of((1 - core) * 8, 8), 8)
-    for d in ARRIVE[1:]:
-        list_in[d].wait_recv()
-    list_sib = []
-    for low, high in ((0, 5), (5, 8)):
-        list_sib.append(send(
-            list_recv.at[pl.ds(low, high - low), other, :],
-            lists.at[pl.ds(SIB[low], high - low)],
-            sibling,
-        ))
-        for p in range(low, high):
-            lists[OWN[p]] = list_recv[p, mine, :]
-
-    source_row = iota((2 * B, CAP), 0)
-    low_row[...] = lax.bitwise_and(iota((1152, B), 0), 1023).astype(jnp.int16)
-
-    def one_hots(s, _):
-        entry = lists[s]
-        row = (entry[1:2, :].astype(I32) - 1) * 256 + entry[2:3, :].astype(I32)
-        select[s] = (entry[0:1, :].astype(I32) == source_row).astype(BF16)
-        low = jnp.broadcast_to(lax.bitwise_and(row, 1023), (16, CAP)).astype(jnp.int16)
-        for side in (0, 1):
-            lanes = pl.ds(pl.multiple_of(s * CAP + side * B, B), B)
-            same = low_row[...] == jnp.tile(low[:, side * B:(side + 1) * B], (72, 1))
-            onehot[:, lanes] = jnp.where(same, jnp.ones((), BF16), jnp.zeros((), BF16))
-        block = jnp.broadcast_to(lax.shift_right_arithmetic(row, 10), (16, CAP))
-        for j in range(NX):
-            factor[s, j] = (block == j).astype(BF16)
-        return 0
-
-    own_first, own_last = (0, 5), (10, 13)
-    lax.fori_loop(*own_first, one_hots, 0)
     wait_for(item_in, 3, -3)
     lax.fori_loop(5, 7, logits, 0)
-    lax.fori_loop(*own_last, one_hots, 0)
     wait_for(item_in, 4, -4)
     lax.fori_loop(7, 8, logits, 0)
 
@@ -246,10 +213,6 @@
         st_send[NX + k:NX + k + 1, :] = total[:, k * B:(k + 1) * B]
     st_send[8:16, :] = jnp.broadcast_to(weight, (8, B))
     stat_in = {d: send(st_send, st_recv.at[d], at_x(d)) for d in (2, 1, 3)}
-    for copy in list_sib:
-        copy.wait_recv()
-    lax.fori_loop(5, 10, one_hots, 0)
-    lax.fori_loop(13, 16, one_hots, 0)
     wait_for(stat_in, 1, 3, 2)
     maxima, factors = [], []
     for k in range(NX):
@@ -313,6 +276,20 @@
         gi_send[p] = gi_own[p].astype(BF16)
         grad_in[d] = send(gi_send.at[p], gi_recv.at[p], at_z(-d))
 
+    mine = pl.ds(pl.multiple_of(core * 8, 8), 8)
+    other = pl.ds(pl.multiple_of((1 - core) * 8, 8), 8)
+    for d in ARRIVE[1:]:
+        list_in[d].wait_recv()
+    list_sib = []
+    for low, high in ((0, 5), (5, 8)):
+        list_sib.append(send(
+            list_recv.at[pl.ds(low, high - low), other, :],
+            lists.at[pl.ds(SIB[low], high - low)],
+            sibling,
+        ))
+        for p in range(low, high):
+            lists[OWN[p]] = list_recv[p, mine, :]
+
     query_grad = gq_own[...]
     for k in (1, 3, 2):
         query_grad_in[k].wait_recv()
@@ -323,28 +300,44 @@
 
     def pooled_slot(half):
         def slot(d, rows):
-            rows = pl.ds(0, E) if rows is None else pl.ds(rows * 64, 64)
-            return pooled.at[OWN[POS[d]], rows, pl.ds(half * B, B)]
+            if rows is None:
+                return pooled.at[half, OWN[POS[d]]]
+            return pooled.at[half, OWN[POS[d]], pl.ds(rows * 64, 64), :]
 
         return slot
 
     def to_sibling(half, low, high):
-        lanes = pl.ds(half * B, B)
         pooled_sib[half, low] = send(
-            pooled.at[pl.ds(OWN[low], high - low), :, lanes],
-            pooled.at[pl.ds(SIB[low], high - low), :, lanes],
-            sibling,
+            pooled.at[half, pl.ds(OWN[low], high - low)], pooled.at[half, pl.ds(SIB[low], high - low)], sibling
         )
 
-    pooled[0, :, 0:B] = dot(wq[...], query_grad, NT_DIMS).astype(BF16)
+    pooled[0, 0] = dot(wq[...], query_grad, NT_DIMS).astype(BF16)
     pooled_in[0] = gather_start(pooled_slot(0), at_y)
     to_sibling(0, 0, 1)
     w_part[0:B, :] = dot(pq[...], query_grad, TN)
 
+    source_row = iota((2 * B, CAP), 0)
+    low_row = lax.bitwise_and(iota((1152, CAP), 0), 1023)
+
+    def one_hots(s, _):
+        entry = lists[s]
+        row = (entry[1:2, :].astype(I32) - 1) * 256 + entry[2:3, :].astype(I32)
+        select[s] = (entry[0:1, :].astype(I32) == source_row).astype(BF16)
+        lanes = pl.ds(pl.multiple_of(s * CAP, CAP), CAP)
+        onehot[:, lanes] = (lax.bitwise_and(row, 1023) == low_row).astype(BF16)
+        block = jnp.broadcast_to(lax.shift_right_arithmetic(row, 10), (16, CAP))
+        for j in range(NX):
+            factor[s, j] = (block == j).astype(BF16)
+        return 0
+
+    lax.fori_loop(0, 5, one_hots, 0)
     gather_pass(pooled_in[0], pooled_slot(0), at_y)
     wait_for(pooled_in[0], 1, -1)
     to_sibling(0, 1, 3)
     to_sibling(0, 3, 5)
+    for copy in list_sib:
+        copy.wait_recv()
+    lax.fori_loop(5, 16, one_hots, 0)
     drain()
 
     item_grad = gi_own[0]
@@ -352,7 +345,7 @@
         grad_in[d].wait_recv()
         item_grad += gi_recv[POS[d]].astype(F32)
     item_grad = item_grad.astype(BF16)
-    pooled[0, :, B:] = dot(wi[...], item_grad, NT_DIMS).astype(BF16)
+    pooled[1, 0] = dot(wi[...], item_grad, NT_DIMS).astype(BF16)
     pooled_in[1] = gather_start(pooled_slot(1), at_y)
     to_sibling(1, 0, 1)
     w_part[B:, :] = dot(pi[...], item_grad, TN)
@@ -364,17 +357,18 @@
     to_sibling(0, 5, 8)
 
     def place_values(s, _):
-        got = dot(pooled[s], select[s]).astype(BF16)
+        got = (dot(pooled[0, s], select[s, 0:B, :]) + dot(pooled[1, s], select[s, B:, :])).astype(BF16)
         lanes = pl.ds(pl.multiple_of(s * CAP, CAP), CAP)
         for j in range(NX):
             values[j * E:(j + 1) * E, lanes] = got * jnp.tile(factor[s, j], (8, 1))
         return 0
 
     def quarter_rows(p):
-        return pl.ds(pl.multiple_of(lax.rem(z + 4 + p * (p + 1), NZ) * B, B), 256)
+        return pl.ds(pl.multiple_of(lax.rem(z + 4 + 3 * p * (p + 1), NZ) * B, B), 256)
 
     def first_part(p, _):
-        t_own[p] = dot(values[:, 0:FIRST], onehot[quarter_rows(p), 0:FIRST], NT_DIMS)
+        part = dot(values[:, 0:FIRST], onehot[quarter_rows(p), 0:FIRST], NT_DIMS)
+        t_own[p] = part.reshape(NX, E, 256)
         return 0
 
     gather_pass(pooled_in[1], pooled_slot(1), at_y)
@@ -386,76 +380,6 @@
         pooled_sib[0, low].wait_recv()
         pooled_sib[1, low].wait_recv()
     lax.fori_loop(5, 10, place_values, 0)
-    wait_for(pooled_in[1], 3, -3, 4, -4)
-    to_sibling(1, 5, 8)
-    lax.fori_loop(0, 2, first_part, 0)
-    pooled_sib[0, 5].wait_recv()
-    pooled_sib[1, 5].wait_recv()
-    lax.fori_loop(10, 16, place_values, 0)
-
-    half_base = len(copies)
-    copies.extend([None] * 8)
-
-    def half_copy(p, side):
-        far = lax.rem(x + 2, NX)
-        rows = pl.ds(pl.multiple_of(far * E + side * 64, 64), 64)
-        return remote(
-            half_base + 2 * p + side, t_send.at[p, rows, :], tx_half.at[p, side], at_x(1 - 2 * side)
-        )
-
-    def send_part(p, part):
-        t_own[p] = part
-        t_send[p] = part.astype(BF16)
-        half_copy(p, 0).start()
-        half_copy(p, 1).start()
-
-    def last_part(p, _):
-        send_part(p, t_own[p] + dot(values[:, FIRST:], onehot[quarter_rows(p), FIRST:], NT_DIMS))
-        return 0
-
-    def whole_part(p, _):
-        send_part(p, dot(values[...], onehot[quarter_rows(p), :], NT_DIMS))
-        return 0
-
-    lax.fori_loop(0, 2, last_part, 0)
-    lax.fori_loop(2, 3, whole_part, 0)
-    for p in range(4):
-        for side in (0, 1):
-            copies[half_base + 2 * p + side] = half_copy(p, side)
-
-    relay_in, tz_in = {}, {}
-
-    def table_relay(p):
-        for side, step in ((0, 1), (1, -1)):
-            copies[half_base + 2 * p + side].wait_recv()
-            near = lax.rem(x + step + NX, NX) * E
-            for half in (0, 1):
-                rows = slice(half * 64, half * 64 + 64)
-                part = t_own[p, pl.ds(pl.multiple_of(near + half * 64, 64), 64), :]
-                if half == side:
-                    part += tx_half[p, side].astype(F32)
-                tx_relay[p, side, rows, :] = part.astype(BF16)
-            relay_in[p, side] = send(tx_relay.at[p, side], tx_recv.at[p, side], at_x(step))
-
-    def table_sum(p):
-        part = t_own[p, pl.ds(pl.multiple_of(x * E, E), E), :]
-        for side in (0, 1):
-            relay_in[p, side].wait_recv()
-            part += tx_recv[p, side].astype(F32)
-        for side in (0, 1):
-            d = (4 + p * (p + 1)) % NZ + side
-            if d == 0:
-                tz_own[...] = part[:, 0:B]
-            else:
-                tz_send[d] = part[:, side * B:(side + 1) * B].astype(BF16)
-                tz_in[d] = send(tz_send.at[d], tz_recv.at[d], at_z(d))
-
-    table_relay(0)
-    table_relay(1)
-    lax.fori_loop(3, 4, whole_part, 0)
-    table_sum(0)
-    table_relay(2)
-    table_sum(1)
 
     w_sum = w_part[pl.ds(pl.multiple_of(x * 64, 64), 64), :]
     for d in (1, 3, 2):
@@ -467,7 +391,122 @@
         to_z = lax.rem(z + d, NZ)
         wz_in[d] = send(wz_send.at[pl.ds(pl.multiple_of(to_z * 8, 8), 8), :], wz_recv.at[d], at_z(d))
 
-    table_relay(3)
+    lax.fori_loop(0, 2, first_part, 0)
+    wait_for(pooled_in[1], 3, -3, 4, -4)
+    to_sibling(1, 5, 8)
+    lax.fori_loop(10, 13, place_values, 0)
+    lax.fori_loop(2, 4, first_part, 0)
+    pooled_sib[0, 5].wait_recv()
+    pooled_sib[1, 5].wait_recv()
+    lax.fori_loop(13, 16, place_values, 0)
+
+    half_base = len(copies)
+    copies.extend([None] * 8)
+
+    def half_copy(p, side):
+        return remote(
+            half_base + 2 * p + side,
+            t_send.at[p, lax.rem(x + 2, NX), pl.ds(side * 48, 48), :],
+            tx_half.at[p, side],
+            at_x(1 - 2 * side),
+        )
+
+    def send_part(p, part):
+        part = t_own[p] + part.reshape(NX, E, 256)
+        t_own[p] = part
+        t_send[p] = part.astype(BF16)
+        half_copy(p, 0).start()
+        half_copy(p, 1).start()
+
+    def last_part(p, _):
+        send_part(p, dot(values[:, FIRST:], onehot[quarter_rows(p), FIRST:], NT_DIMS))
+        return 0
+
+    lax.fori_loop(0, 4, last_part, 0)
+    for p in range(4):
+        for side in (0, 1):
+            copies[half_base + 2 * p + side] = half_copy(p, side)
+
+    def low_columns(p, side):
+        return t_send.at[p, :, pl.ds(96, 32), pl.ds(side * B, B)]
+
+    low_half = [
+        send(t_send.at[0, pl.ds(2 * side, 2), pl.ds(96, 32), pl.ds(0, B)], lz_half.at[side], at_z(2 - 4 * side))
+        for side in (0, 1)
+    ]
+    low_relay = [
+        send(low_columns(1, 1), lz_relay.at[0], at_z(1)),
+        send(low_columns(0, 1), lz_relay.at[1], at_z(-1)),
+    ]
+    low_in = [
+        send(low_columns(3, 1), lz_recv.at[0], at_z(1)),
+        send(low_columns(2, 1), lz_recv.at[1], at_z(-1)),
+    ]
+
+    def low_pass():
+        for side in (0, 1):
+            low_relay[side].wait_recv()
+            low_half[side].wait_recv()
+            lz_own[side] = t_own[1 + side, :, 96:, 0:B] + lz_relay[side].astype(F32)
+            pair_of = slice(2 * side, 2 * side + 2)
+            lz_own[side, pair_of] += lz_half[side].astype(F32)
+            lz_send[side] = lz_own[side].astype(BF16)
+            low_in.append(send(lz_send.at[side], lz_recv.at[2 + side], at_z(2 - 4 * side)))
+
+    low_x = {}
+
+    def low_sum():
+        part = t_own[3, :, 96:, 0:B]
+        for k in range(4):
+            low_in[k].wait_recv()
+            part += lz_recv[k].astype(F32)
+        lz_own[2] = part
+        lx_send[...] = part.astype(BF16)
+        for d in (2, 1, 3):
+            low_x[d] = send(lx_send.at[lax.rem(x + d, NX)], lx_recv.at[d], at_x(d))
+
+    relay_in, tz_half_in, tz_relay_in, tz_in = {}, {}, {}, {}
+
+    def table_relay(p):
+        for side, step in ((0, 1), (1, -1)):
+            copies[half_base + 2 * p + side].wait_recv()
+            near = lax.rem(x + step + NX, NX)
+            for half in (0, 1):
+                rows = slice(half * 48, half * 48 + 48)
+                part = t_own[p, near, rows, :]
+                if half == side:
+                    part += tx_half[p, side].astype(F32)
+                tx_relay[p, side, rows, :] = part.astype(BF16)
+            relay_in[p, side] = send(tx_relay.at[p, side], tx_recv.at[p, side], at_x(step))
+
+    def table_sum(p):
+        part = t_own[p, x, 0:96, :]
+        for side in (0, 1):
+            relay_in[p, side].wait_recv()
+            part += tx_recv[p, side].astype(F32)
+        tz_send[p] = part[:, B:].astype(BF16)
+        if p == 0:
+            tz_first[...] = part[:, 0:B].astype(BF16)
+            for side in (0, 1):
+                tz_half_in[side] = send(
+                    tz_first.at[pl.ds(side * 48, 48), :], tz_half.at[side], at_z(2 - 4 * side)
+                )
+        else:
+            tz_own[p - 1] = part[:, 0:B]
+        if p < 2:
+            tz_relay_in[1 - p] = send(tz_send.at[p], tz_relay.at[1 - p], at_z(2 * p - 1))
+        else:
+            tz_in[3 - p] = send(tz_send.at[p], tz_recv.at[3 - p], at_z(2 * p - 5))
+
+    def table_pass():
+        for side in (0, 1):
+            tz_relay_in[side].wait_recv()
+            tz_half_in[side].wait_recv()
+            rows = slice(side * 48, side * 48 + 48)
+            tz_own[side] += tz_relay[side].astype(F32)
+            tz_own[side, rows, :] += tz_half[side].astype(F32)
+            tz_back[side] = tz_own[side].astype(BF16)
+            tz_in[2 + side] = send(tz_back.at[side], tz_recv.at[2 + side], at_z(2 - 4 * side))
 
     w_sum = wz_send[pl.ds(pl.multiple_of(z * 8, 8), 8), :]
     for d in ARRIVE[1:]:
@@ -476,22 +515,61 @@
     wy_recv[0, 0] = w_sum
     wy_in = {d: send(wy_recv.at[0, 0], wy_recv.at[0, d], at_y(d)) for d in ARRIVE[1:]}
 
+    table_relay(0)
+    table_relay(1)
+    table_sum(0)
+    low_pass()
+
+    for d in ARRIVE[1:]:
+        wy_in[d].wait_recv()
+    wy_sib = send(wy_recv.at[0], wy_recv.at[1], sibling)
+    table_relay(2)
+    table_sum(1)
+
+    wy_sib.wait_recv()
+    w_sum = wy_recv[0, 0]
+    for d in range(1, NY):
+        w_sum += wy_recv[0, d]
+    for d in range(NY):
+        w_sum += wy_recv[1, d]
+
+    def w_rows(place):
+        return gw_ref.at[pl.ds(pl.multiple_of(place * 8, 8), 8), :]
+
+    gw_ref[pl.ds(pl.multiple_of(dp * 8, 8), 8), :] = w_sum
+    w_back = {d: send(w_rows(dp), w_rows(dp), at_z(d)) for d in ARRIVE[1:]}
+
+    table_relay(3)
     table_sum(2)
+    low_sum()
+    table_pass()
+    table_sum(3)
     drain()
-    table_sum(3)
-
-    part = tz_own[...]
-    for d in (4, 5, 6, 7, 2, 3, 1):
-        tz_in[d].wait_recv()
-        part += tz_recv[d].astype(F32)
-    t_back[x, 0] = part.T.astype(BF16)
+
+    low = lz_own[2, x]
+    for d in (1, 3, 2):
+        low_x[d].wait_recv()
+        low += lx_recv[d].astype(F32)
+    part = tz_own[2]
+    for k in (1, 0, 2, 3):
+        tz_in[k].wait_recv()
+        part += tz_recv[k].astype(F32)
+    rows = jnp.concatenate([part, low], axis=0).T.astype(BF16)
+    t_back[x, 0] = rows[0:96]
+    l_back[0, x] = rows[96:]
 
     def back_slot(d, half):
         if half is None:
             return t_back.at[x, POS[d]]
-        return t_back.at[x, POS[d], pl.ds(half * 64, 64), :]
+        return t_back.at[x, POS[d], pl.ds(half * 48, 48), :]
+
+    def low_slot(d, half):
+        if half is None:
+            return l_back.at[POS[d]]
+        return l_back.at[POS[d], pl.ds(2 * half, 2)]
 
     back = gather_start(back_slot, at_z)
+    low_back = [send(l_back.at[0, x], l_back.at[0, x], at_x(d)) for d in (2, 1, 3)]
     near_in, far_in = {}, []
 
     def to_near(low, high):
@@ -505,51 +583,51 @@
             near_in[low, side].wait_recv()
             held = lax.rem(x - step + NX, NX)
             if middle is None:
-                rows = t_back.at[held, pl.ds(low, high - low), pl.ds(side * 64, 64), :]
+                rows = t_back.at[held, pl.ds(low, high - low), pl.ds(side * 48, 48), :]
             else:
                 rows = t_back.at[held, low + side]
             far_in.append(send(rows, rows, at_x(step)))
 
     to_near(0, 1)
-
-    for d in ARRIVE[1:]:
-        wy_in[d].wait_recv()
-    wy_sib = send(wy_recv.at[0], wy_recv.at[1], sibling)
-    gather_pass(back, back_slot, at_z)
-    to_near(1, 3)
-    to_far(0, 1)
-    wait_for(back, 1, -1)
-    to_near(3, 5)
-    wy_sib.wait_recv()
-    w_sum = wy_recv[0, 0]
-    for d in range(1, NY):
-        w_sum += wy_recv[0, d]
-    for d in range(NY):
-        w_sum += wy_recv[1, d]
-
-    def w_rows(place):
-        return gw_ref.at[pl.ds(pl.multiple_of(place * 8, 8), 8), :]
-
-    gw_ref[pl.ds(pl.multiple_of(dp * 8, 8), 8), :] = w_sum
-    w_back = {d: send(w_rows(dp), w_rows(dp), at_z(d)) for d in ARRIVE[1:]}
-    to_far(1, 3)
-    wait_for(back, 3, -3, 4, -4)
-    to_near(5, 8)
-    to_far(3, 5)
-
-    def rows_of(far, p, d):
-        place = far * NZ + lax.rem(z - d + NZ, NZ)
-        table_ref[pl.ds(pl.multiple_of(place * B, B), B), :] = t_back[far, p]
 
     wait_for(w_back, *ARRIVE[1:])
     w_held = gw_ref.at[pl.ds(pl.multiple_of(x * 64, 64), 64), :]
     for step in (2, 1, 3):
         far_in.append(send(w_held, w_held, at_x(step)))
+
+
+    gather_pass(back, back_slot, at_z)
+    to_near(1, 3)
+    for copy in low_back:
+        copy.wait_recv()
+    low_back = gather_start(low_slot, at_z)
+    to_far(0, 1)
+    wait_for(back, 1, -1)
+    to_near(3, 5)
+    to_far(1, 3)
+    wait_for(back, 3, -3, 4, -4)
+    to_near(5, 8)
+    gather_pass(low_back, low_slot, at_z)
+    to_far(3, 5)
+
+    def rows_of(far, p, d):
+        place = (far * NZ + lax.rem(z - d + NZ, NZ)) * B
+        table_ref[pl.ds(pl.multiple_of(place, B), 96), :] = t_back[far, p]
+
+    def low_rows_of(p, d):
+        for far in range(NX):
+            place = (far * NZ + lax.rem(z - d + NZ, NZ)) * B + 96
+            table_ref[pl.ds(pl.multiple_of(place, 32), 32), :] = l_back[p, far]
+
     to_far(5, 8)
     for p, d in enumerate(ARRIVE):
         rows_of(x, p, d)
         rows_of(lax.rem(x + 1, NX), p, d)
         rows_of(lax.rem(x + 3, NX), p, d)
+    wait_for(low_back, 1, -1, 3, -3, 4, -4)
+    for p, d in enumerate(ARRIVE):
+        low_rows_of(p, d)
+    drain()
     for copy in far_in:
         copy.wait_recv()
     for p, d in enumerate(ARRIVE):
@@ -557,13 +635,19 @@
     drain()
 
 
-def finish(table_ref, gw_ref, out_ref, gwq_ref, gwi_ref):
-    out_ref[...] = table_ref[...].astype(F32)
-
-    @pl.when(pl.program_id(0) == 0)
-    def _():
-        gwq_ref[...] = gw_ref[0:B, :]
-        gwi_ref[...] = gw_ref[B:, :]
+def finish(table_ref, gw_ref, out_ref, gwq_ref, gwi_ref, wide, sem):
+    copies = [
+        pltpu.make_async_copy(gw_ref.at[pl.ds(0, B), :], gwq_ref, sem.at[8]),
+        pltpu.make_async_copy(gw_ref.at[pl.ds(B, B), :], gwi_ref, sem.at[9]),
+    ]
+    for copy in copies:
+        copy.start()
+    for i in range(8):
+        wide[i] = table_ref[i * 512:(i + 1) * 512, :].astype(F32)
+        copies.append(pltpu.make_async_copy(wide.at[i], out_ref.at[pl.ds(i * 512, 512), :], sem.at[i]))
+        copies[-1].start()
+    for copy in copies:
+        copy.wait()
 
 
 def on_device(q, it, pq, pi, wq, wi, pw, owner, row):
@@ -608,26 +692,37 @@
             vmem(B, CAP),
             vmem(NY, 16, CAP),
             vmem(NT, 8, CAP),
-            vmem(1152, B, dtype=jnp.int16),
             vmem(1152, NT * CAP, dtype=BF16),
             vmem(NT, 2 * B, CAP, dtype=BF16),
             vmem(NT, NX, 16, CAP, dtype=BF16),
-            vmem(NT, E, 2 * B, dtype=BF16),
+            vmem(2, NT, E, B, dtype=BF16),
             vmem(NX * E, NT * CAP, dtype=BF16),
             vmem(2 * B, W),
             vmem(NX, 64, W),
             vmem(64, W),
             vmem(NZ, 8, W),
             vmem(2, NY, 8, W),
-            vmem(4, NX * E, 256),
-            vmem(4, NX * E, 256, dtype=BF16),
-            vmem(4, 2, 64, 256, dtype=BF16),
-            vmem(4, 2, E, 256, dtype=BF16),
-            vmem(4, 2, E, 256, dtype=BF16),
-            vmem(E, B),
-            vmem(NZ, E, B, dtype=BF16),
-            vmem(NZ, E, B, dtype=BF16),
-            vmem(NX, NZ, B, E, dtype=BF16),
+            vmem(4, NX, E, 256),
+            vmem(4, NX, E, 256, dtype=BF16),
+            vmem(4, 2, 48, 256, dtype=BF16),
+            vmem(4, 2, 96, 256, dtype=BF16),
+            vmem(4, 2, 96, 256, dtype=BF16),
+            vmem(96, B, dtype=BF16),
+            vmem(3, 96, B),
+            vmem(4, 96, B, dtype=BF16),
+            vmem(2, 48, B, dtype=BF16),
+            vmem(2, 96, B, dtype=BF16),
+            vmem(2, 96, B, dtype=BF16),
+            vmem(4, 96, B, dtype=BF16),
+            vmem(2, 2, 32, B, dtype=BF16),
+            vmem(2, NX, 32, B, dtype=BF16),
+            vmem(3, NX, 32, B),
+            vmem(2, NX, 32, B, dtype=BF16),
+            vmem(4, NX, 32, B, dtype=BF16),
+            vmem(NX, 32, B, dtype=BF16),
+            vmem(NX, 32, B, dtype=BF16),
+            vmem(NX, NZ, 96, E, dtype=BF16),
+            vmem(NZ, NX, 32, E, dtype=BF16),
             pltpu.SemaphoreType.DMA((9,)),
             pltpu.SemaphoreType.DMA((N_COPIES,)),
             pltpu.SemaphoreType.DMA((N_COPIES,)),
@@ -641,21 +736,17 @@
             q, it, pq, pi, wq, wi, pw.reshape(1, B), owner.reshape(B, 16).T, row.reshape(B, 16).T
         )
     ])
-    whole_w = pl.BlockSpec((B, W), lambda i: (0, 0))
     return pl.pallas_call(
         finish,
-        grid=(4,),
         out_shape=(
             jax.ShapeDtypeStruct((4096, E), F32),
             jax.ShapeDtypeStruct((B, W), F32),
             jax.ShapeDtypeStruct((B, W), F32),
         ),
-        in_specs=[
-            pl.BlockSpec((1024, E), lambda i: (i, 0)),
-            pl.BlockSpec((2 * B, W), lambda i: (0, 0)),
-        ],
-        out_specs=(pl.BlockSpec((1024, E), lambda i: (i, 0)), whole_w, whole_w),
-        compiler_params=pltpu.CompilerParams(vmem_limit_bytes=8 * 1024 * 1024),
+        in_specs=[pl.BlockSpec(memory_space=pltpu.VMEM)] * 2,
+        out_specs=(pl.BlockSpec(memory_space=pltpu.HBM),) * 3,
+        scratch_shapes=[vmem(8, 512, E), pltpu.SemaphoreType.DMA((10,))],
+        compiler_params=pltpu.CompilerParams(vmem_limit_bytes=12 * 1024 * 1024),
     )(table, gw)
 
 

time: 99.4 us -> 92.5 us (0.931)
  the two profiles are of different devices: /device:TPU:2 before, /device:TPU:4 now
where the time goes in v2:
time: 92.5 us; the launch traced here: 92.4 us
  Pallas kernels  91.7 us (99%)
    pallas_call x1, Pallas kernels, on_device(): pl.pallas_call(kernel, out_shape=(jax.ShapeDtypeStruct((4096, E), BF16),...  90.2 us

profile of v2, /device:TPU:4, one launch (start us, length us, event | category | flops | bytes accessed | tf_op | source)
XLA Modules:
  0.0 92.4 jit_solution(14030021995130949990)
XLA Ops:
  0.6 90.2 %shard_map.112 = (bf16[4096,128]{1,0:T(8,128)(2,1)S(1)}, f32[256,256]{1,0:T(8,128)S(1)}) custom-call(bf16[128,256]{1,0:T(8,128)(2,1)} %q_ref.1, bf16[128,256]{1,0:T(8,128)(2,1)} %it_ref.1, bf16[128,128]{1,0:T(8,128)(2,1)} %pq_ref.1, bf16[128,128]{1,0:T(8,128)(2,1)} %pi_ref.1, bf16[128,256]{1,0:T(8,128)(2,1)} %wq_ref.1, bf16[128,256]{1,0:T(8,128)(2,1)} %wi_ref.1, ...), custom_call_target="tpu_custom_call" | custom-call | tf_op jit(solution)/shard_map/pallas_call | solution.py:657
  90.9 1.5 %shard_map.113 = (f32[4096,128]{1,0:T(8,128)}, f32[128,256]{1,0:T(8,128)}, f32[128,256]{1,0:T(8,128)}) custom-call(bf16[4096,128]{1,0:T(8,128)(2,1)S(1)} %get-tuple-element.5.table_ref, f32[256,256]{1,0:T(8,128)S(1)} %get-tuple-element.6.gw_ref), custom_call_target="tpu_custom_call" | custom-call | tf_op jit(solution)/shard_map/pallas_call | solution.py:739

commit v3 on v2

--- a/solution.py
+++ b/solution.py
@@ -31,6 +31,7 @@
 
 ARRIVE = (0, 2, 6, 1, 7, 3, 5, 4)
 POS = {d: p for p, d in enumerate(ARRIVE)}
+RING = {d: p for p, d in enumerate((0, 1, 7, 2, 6, 3, 5, 4))}
 OWN = (0, 1, 2, 3, 4, 10, 11, 12)
 SIB = (5, 6, 7, 8, 9, 13, 14, 15)
 FIRST = 10 * CAP
@@ -41,9 +42,9 @@
     table_ref, gw_ref,
     pq, pi, wq, wi, pw, ow, rw,
     ibuf, qbuf, ebuf, gbuf, tops, totals, st_send, st_recv,
-    gi_send, gi_relay, gi_half, gi_recv, gi_own, gq_send, gq_recv, gq_own,
-    taken, slots_a, slots_b, list_send, list_recv, lists, onehot, select, factor, pooled, values,
-    w_part, wx_recv, wz_send, wz_recv, wy_recv,
+    gi_send, gi_sum, gi_own, gq_send, gq_recv, gq_own,
+    taken, slots_a, slots_b, lists, onehot, select, factor, pooled, values,
+    w_part, wx_recv, wz_send, wz_relay, wz_pass, wz_recv, wy_recv, w_own,
     t_own, t_send, tx_half, tx_relay, tx_recv, tz_first, tz_own, tz_send, tz_half, tz_relay, tz_back, tz_recv,
     lz_half, lz_relay, lz_own, lz_send, lz_recv, lx_send, lx_recv, t_back, l_back,
     load_sem, send_sem, recv_sem,
@@ -64,8 +65,8 @@
     sibling = (dp, tb + 1 - 2 * core)
     partners = (
         [at_x(d) for d in range(1, NX)]
-        + [at_z(d) for d in range(1, NZ)]
-        + [at_y(d) for d in range(1, NY)]
+        + [at_z(d) for d in (1, 2, -1, -2)]
+        + [at_y(d) for d in (1, 2, -1, -2)]
         + [sibling]
     )
     barrier = pltpu.get_barrier_semaphore()
@@ -128,12 +129,24 @@
         for name in names:
             got[name].wait_recv()
 
-    def item_slot(d, half):
-        if half is None:
-            return ibuf.at[pl.ds(POS[d] * B, B), :]
-        return ibuf.at[pl.ds(POS[d] * B + half * 64, 64), :]
-
-    item_in = gather_start(item_slot, at_z, it_ref)
+    def item_half(d, half):
+        return ibuf.at[pl.ds(RING[d] * B + half * 64, 64), :]
+
+    item_in = {}
+    for up in (0, 1):
+        item_in[1, up] = send(it_ref.at[pl.ds(up * 64, 64), :], item_half(1, up), at_z(1))
+        item_in[7, 1 - up] = send(it_ref.at[pl.ds(64 - up * 64, 64), :], item_half(7, 1 - up), at_z(-1))
+
+    def item_step(k):
+        for up in (0, 1):
+            down = 1 - up
+            item_in[k, up].wait_recv()
+            if k < 3 or up == 0:
+                item_in[k + 1, up] = send(item_half(k, up), item_half(k + 1, up), at_z(1))
+            item_in[8 - k, down].wait_recv()
+            if k < 3 or down == 1:
+                item_in[7 - k, down] = send(item_half(8 - k, down), item_half(7 - k, down), at_z(-1))
+
     query_in = {}
     for d in (1, 3, 2):
         query_in[d] = send(q_ref, qbuf.at[pl.ds(d * B, B), :], at_x(d))
@@ -150,8 +163,9 @@
         lax.shift_right_logical(at_col, 4) < lax.shift_right_logical(at_row, 4),
     ).astype(BF16)
     taken[...] = (counts[:, 0:B] + dot(earlier, counts[:, B:].astype(BF16))) * hits
-    list_row = iota((B, B), 0)
-    list_owner, piece = lax.shift_right_logical(list_row, 3), lax.bitwise_and(list_row, 7)
+    item_step(1)
+    list_row = iota((64, B), 0)
+    list_owner, piece = lax.bitwise_and(list_row, 15), lax.shift_right_logical(list_row, 4)
     pair = iota((1, B), 1)
     place = iota((CAP, B), 0)
 
@@ -174,16 +188,15 @@
         return 0
 
     lax.fori_loop(0, 16, list_slot, 0)
-    list_send[...] = dot(slots_a[...], slots_b[...], NT_DIMS)
-    list_in = {}
-    for d in ARRIVE[1:]:
-        to_y = lax.rem(y + d, NY)
-        list_in[d] = send(
-            list_send.at[pl.ds(pl.multiple_of(to_y * 16, 16), 16), :], list_recv.at[POS[d]], at_y(d)
-        )
-    list_recv[0] = list_send[pl.ds(pl.multiple_of(y * 16, 16), 16), :]
-
-    gather_pass(item_in, item_slot, at_z)
+    lists[0] = dot(slots_a[...], slots_b[...], NT_DIMS).astype(BF16)
+
+    def list_slot_of(d, half):
+        if half is None:
+            return lists.at[OWN[POS[d]]]
+        return lists.at[OWN[POS[d]], pl.ds(half * 32, 32), :]
+
+    list_in = gather_start(list_slot_of, at_y)
+    item_step(2)
 
     wait_for(query_in, 1, 3, 2)
 
@@ -197,12 +210,10 @@
         totals[pl.ds(p, 1), :] = jnp.sum(block, axis=0, keepdims=True)
         return 0
 
-    wait_for(item_in, 1, -1)
-    lax.fori_loop(0, 5, logits, 0)
-
-    wait_for(item_in, 3, -3)
-    lax.fori_loop(5, 7, logits, 0)
-    wait_for(item_in, 4, -4)
+    lax.fori_loop(0, 3, logits, 0)
+    item_step(3)
+    lax.fori_loop(3, 7, logits, 0)
+    wait_for(item_in, (4, 0), (4, 1))
     lax.fori_loop(7, 8, logits, 0)
 
     top = jnp.max(tops[...], axis=0, keepdims=True)
@@ -213,6 +224,7 @@
         st_send[NX + k:NX + k + 1, :] = total[:, k * B:(k + 1) * B]
     st_send[8:16, :] = jnp.broadcast_to(weight, (8, B))
     stat_in = {d: send(st_send, st_recv.at[d], at_x(d)) for d in (2, 1, 3)}
+    gather_pass(list_in, list_slot_of, at_y)
     wait_for(stat_in, 1, 3, 2)
     maxima, factors = [], []
     for k in range(NX):
@@ -236,27 +248,29 @@
         gbuf[rows, :] = block
         return SCALE * dot(block, qbuf[...])
 
-    def far_terms(p, _):
-        gi_send[p] = item_terms(p).astype(BF16)
-        return 0
-
     def near_terms(p, _):
         gi_own[p] = item_terms(p)
         return 0
 
-    lax.fori_loop(7, 8, far_terms, 0)
-    half_in = [
-        send(gi_send.at[7, pl.ds(0, 64), :], gi_half.at[0], at_z(2)),
-        send(gi_send.at[7, pl.ds(64, 64), :], gi_half.at[1], at_z(-2)),
-    ]
-    lax.fori_loop(5, 7, far_terms, 0)
-    relay_in = [
-        send(gi_send.at[POS[5]], gi_relay.at[0], at_z(1)),
-        send(gi_send.at[POS[3]], gi_relay.at[1], at_z(-1)),
-    ]
-    lax.fori_loop(3, 5, far_terms, 0)
-    grad_in = {d: send(gi_send.at[POS[d]], gi_recv.at[POS[d]], at_z(-d)) for d in (7, 1)}
-    lax.fori_loop(0, 3, near_terms, 0)
+    sum_in = {}
+    half_of = (slice(0, 64), slice(64, 128))
+
+    def send_sum(way, k, half):
+        p = RING[(4, 5, 6, 7)[k] if way == 0 else (4, 3, 2, 1)[k]]
+        block = gi_own[p, half_of[half], :]
+        if (way, k - 1, half) in sum_in:
+            sum_in[way, k - 1, half].wait_recv()
+            block += gi_sum[way, k - 1, half].astype(F32)
+        gi_send[way, k, half] = block.astype(BF16)
+        sum_in[way, k, half] = send(gi_send.at[way, k, half], gi_sum.at[way, k, half], at_z(1 - 2 * way))
+
+    near_terms(7, 0)
+    send_sum(0, 0, 0)
+    send_sum(1, 0, 1)
+    lax.fori_loop(5, 7, near_terms, 0)
+    send_sum(0, 1, 1)
+    send_sum(1, 1, 0)
+    lax.fori_loop(0, 5, near_terms, 0)
     same = iota((B, B), 0) == iota((B, B), 1)
     diagonal = ebuf[0:B, 0:B] * totals[0:1, 0:B] - jnp.where(same, weight, 0.0)
     gbuf[0:B, 0:B] = diagonal.astype(BF16)
@@ -267,62 +281,37 @@
     for k in range(1, NX):
         gq_send[k] = terms[k * B:(k + 1) * B, :].astype(BF16)
     query_grad_in = {k: send(gq_send.at[k], gq_recv.at[k], at_x(-k)) for k in (2, 1, 3)}
-    for side, (d, rows) in enumerate(((6, slice(0, 64)), (2, slice(64, 128)))):
-        p = POS[d]
-        relay_in[side].wait_recv()
-        half_in[side].wait_recv()
-        gi_own[p] += gi_relay[side].astype(F32)
-        gi_own[p, rows, :] += gi_half[side].astype(F32)
-        gi_send[p] = gi_own[p].astype(BF16)
-        grad_in[d] = send(gi_send.at[p], gi_recv.at[p], at_z(-d))
-
-    mine = pl.ds(pl.multiple_of(core * 8, 8), 8)
-    other = pl.ds(pl.multiple_of((1 - core) * 8, 8), 8)
-    for d in ARRIVE[1:]:
-        list_in[d].wait_recv()
+    send_sum(0, 1, 0)
+    send_sum(1, 1, 1)
+    send_sum(0, 2, 1)
+    send_sum(1, 2, 0)
+
     list_sib = []
-    for low, high in ((0, 5), (5, 8)):
+
+    def lists_to_sibling(low, high):
         list_sib.append(send(
-            list_recv.at[pl.ds(low, high - low), other, :],
-            lists.at[pl.ds(SIB[low], high - low)],
-            sibling,
+            lists.at[pl.ds(OWN[low], high - low)], lists.at[pl.ds(SIB[low], high - low)], sibling
         ))
-        for p in range(low, high):
-            lists[OWN[p]] = list_recv[p, mine, :]
-
-    query_grad = gq_own[...]
-    for k in (1, 3, 2):
-        query_grad_in[k].wait_recv()
-        query_grad += gq_recv[k].astype(F32)
-    query_grad = query_grad.astype(BF16)
-
-    pooled_in, pooled_sib = {}, {}
-
-    def pooled_slot(half):
-        def slot(d, rows):
-            if rows is None:
-                return pooled.at[half, OWN[POS[d]]]
-            return pooled.at[half, OWN[POS[d]], pl.ds(rows * 64, 64), :]
-
-        return slot
-
-    def to_sibling(half, low, high):
-        pooled_sib[half, low] = send(
-            pooled.at[half, pl.ds(OWN[low], high - low)], pooled.at[half, pl.ds(SIB[low], high - low)], sibling
-        )
-
-    pooled[0, 0] = dot(wq[...], query_grad, NT_DIMS).astype(BF16)
-    pooled_in[0] = gather_start(pooled_slot(0), at_y)
-    to_sibling(0, 0, 1)
-    w_part[0:B, :] = dot(pq[...], query_grad, TN)
-
+
+    wait_for(list_in, 1, -1, 3, -3, 4, -4)
+    lists_to_sibling(0, 5)
+    lists_to_sibling(5, 8)
+    send_sum(0, 2, 0)
+    send_sum(1, 2, 1)
+    send_sum(0, 3, 1)
+    send_sum(1, 3, 0)
     source_row = iota((2 * B, CAP), 0)
+    owner_row = iota((NT, CAP), 0)
     low_row = lax.bitwise_and(iota((1152, CAP), 0), 1023)
 
     def one_hots(s, _):
-        entry = lists[s]
-        row = (entry[1:2, :].astype(I32) - 1) * 256 + entry[2:3, :].astype(I32)
-        select[s] = (entry[0:1, :].astype(I32) == source_row).astype(BF16)
+        entry = lists[s].astype(F32)
+        source, high, low = [
+            jnp.sum(jnp.where(owner_row == tb, entry[16 * k:16 * k + 16, :], 0.0), axis=0, keepdims=True).astype(I32)
+            for k in range(3)
+        ]
+        row = (high - 1) * 256 + low
+        select[s] = (source == source_row).astype(BF16)
         lanes = pl.ds(pl.multiple_of(s * CAP, CAP), CAP)
         onehot[:, lanes] = (lax.bitwise_and(row, 1023) == low_row).astype(BF16)
         block = jnp.broadcast_to(lax.shift_right_arithmetic(row, 10), (16, CAP))
@@ -331,30 +320,60 @@
         return 0
 
     lax.fori_loop(0, 5, one_hots, 0)
+    lax.fori_loop(10, 13, one_hots, 0)
+    send_sum(0, 3, 0)
+    send_sum(1, 3, 1)
+
+    query_grad = gq_own[...]
+    for k in (1, 3, 2):
+        query_grad_in[k].wait_recv()
+        query_grad += gq_recv[k].astype(F32)
+    query_grad = query_grad.astype(BF16)
+
+    pooled_in, pooled_sib = {}, {}
+
+    def pooled_slot(half):
+        def slot(d, rows):
+            if rows is None:
+                return pooled.at[half, OWN[POS[d]]]
+            return pooled.at[half, OWN[POS[d]], pl.ds(rows * 64, 64), :]
+
+        return slot
+
+    def to_sibling(half, low, high):
+        pooled_sib[half, low] = send(
+            pooled.at[half, pl.ds(OWN[low], high - low)], pooled.at[half, pl.ds(SIB[low], high - low)], sibling
+        )
+
+    pooled[0, 0] = dot(wq[...], query_grad, NT_DIMS).astype(BF16)
+    pooled_in[0] = gather_start(pooled_slot(0), at_y)
+    to_sibling(0, 0, 1)
+    w_part[0:B, :] = dot(pq[...], query_grad, TN)
+
+    for copy in list_sib:
+        copy.wait_recv()
+    lax.fori_loop(5, 10, one_hots, 0)
+    lax.fori_loop(13, 16, one_hots, 0)
+    drain()
+
+    item_grad = gi_own[0]
+    for way in (0, 1):
+        for half in (0, 1):
+            sum_in[way, 3, half].wait_recv()
+        item_grad += gi_sum[way, 3].reshape(B, W).astype(F32)
+    item_grad = item_grad.astype(BF16)
+    pooled[1, 0] = dot(wi[...], item_grad, NT_DIMS).astype(BF16)
+    pooled_in[1] = gather_start(pooled_slot(1), at_y)
+    to_sibling(1, 0, 1)
     gather_pass(pooled_in[0], pooled_slot(0), at_y)
     wait_for(pooled_in[0], 1, -1)
     to_sibling(0, 1, 3)
     to_sibling(0, 3, 5)
-    for copy in list_sib:
-        copy.wait_recv()
-    lax.fori_loop(5, 16, one_hots, 0)
-    drain()
-
-    item_grad = gi_own[0]
-    for d in (1, 7, 2, 6):
-        grad_in[d].wait_recv()
-        item_grad += gi_recv[POS[d]].astype(F32)
-    item_grad = item_grad.astype(BF16)
-    pooled[1, 0] = dot(wi[...], item_grad, NT_DIMS).astype(BF16)
-    pooled_in[1] = gather_start(pooled_slot(1), at_y)
-    to_sibling(1, 0, 1)
     w_part[B:, :] = dot(pi[...], item_grad, TN)
     w_in = {}
     for d in (2, 1, 3):
         to_x = lax.rem(x + d, NX)
         w_in[d] = send(w_part.at[pl.ds(pl.multiple_of(to_x * 64, 64), 64), :], wx_recv.at[d], at_x(d))
-    wait_for(pooled_in[0], 3, -3, 4, -4)
-    to_sibling(0, 5, 8)
 
     def place_values(s, _):
         got = (dot(pooled[0, s], select[s, 0:B, :]) + dot(pooled[1, s], select[s, B:, :])).astype(BF16)
@@ -386,16 +405,29 @@
         w_in[d].wait_recv()
         w_sum += wx_recv[d]
     wz_send[...] = w_sum
+
+    def w_chunk(d):
+        return pl.ds(pl.multiple_of(lax.rem(z + d + NZ, NZ) * 8, 8), 8)
+
     wz_in = {}
-    for d in ARRIVE[1:]:
-        to_z = lax.rem(z + d, NZ)
-        wz_in[d] = send(wz_send.at[pl.ds(pl.multiple_of(to_z * 8, 8), 8), :], wz_recv.at[d], at_z(d))
+    for d, via, dst in (
+        (4, 2, wz_relay.at[0]), (3, 1, wz_relay.at[1]), (-3, -1, wz_relay.at[2]),
+        (1, 1, wz_recv.at[0]), (-1, -1, wz_recv.at[1]),
+    ):
+        wz_in[d] = send(wz_send.at[w_chunk(d), :], dst, at_z(via))
 
     lax.fori_loop(0, 2, first_part, 0)
+    wait_for(pooled_in[0], 3, -3, 4, -4)
+    to_sibling(0, 5, 8)
     wait_for(pooled_in[1], 3, -3, 4, -4)
     to_sibling(1, 5, 8)
     lax.fori_loop(10, 13, place_values, 0)
     lax.fori_loop(2, 4, first_part, 0)
+    wait_for(wz_in, 4, 3, -3)
+    wz_pass[0] = wz_send[w_chunk(2), :] + wz_relay[0] + wz_relay[1]
+    wz_pass[1] = wz_send[w_chunk(-2), :] + wz_relay[2]
+    for side, d in ((0, 2), (1, -2)):
+        wz_in[d] = send(wz_pass.at[side], wz_recv.at[2 + side], at_z(d))
     pooled_sib[0, 5].wait_recv()
     pooled_sib[1, 5].wait_recv()
     lax.fori_loop(13, 16, place_values, 0)
@@ -508,23 +540,40 @@
             tz_back[side] = tz_own[side].astype(BF16)
             tz_in[2 + side] = send(tz_back.at[side], tz_recv.at[2 + side], at_z(2 - 4 * side))
 
-    w_sum = wz_send[pl.ds(pl.multiple_of(z * 8, 8), 8), :]
-    for d in ARRIVE[1:]:
-        wz_in[d].wait_recv()
-        w_sum += wz_recv[d]
-    wy_recv[0, 0] = w_sum
-    wy_in = {d: send(wy_recv.at[0, 0], wy_recv.at[0, d], at_y(d)) for d in ARRIVE[1:]}
+    def small_pass(got, slot, at, there):
+        got[2].wait_recv()
+        got[3] = send(slot(2), there(2, 3), at(1))
+        got[4] = send(slot(2), there(2, 4), at(2))
+        got[-2].wait_recv()
+        got[5] = send(slot(-2), there(-2, 5), at(-1))
+
+    def wy_slot(d):
+        return wy_recv.at[0, d % 8]
+
+    def w_rows(d):
+        place = x * NZ + lax.rem(z - d + NZ, NZ)
+        return gw_ref.at[pl.ds(pl.multiple_of(place * 8, 8), 8), pl.ds(pl.multiple_of(core * B, B), B)]
 
     table_relay(0)
     table_relay(1)
+    w_sum = wz_send[w_chunk(0), :]
+    wait_for(wz_in, 1, -1, 2, -2)
+    for k in range(4):
+        w_sum += wz_recv[k]
+    wy_recv[0, 0] = w_sum
+    wy_in = {d: send(wy_slot(0), wy_slot(d), at_y(d)) for d in (2, -2, 1, -1)}
+
     table_sum(0)
     low_pass()
-
-    for d in ARRIVE[1:]:
-        wy_in[d].wait_recv()
+    table_relay(2)
+    small_pass(wy_in, wy_slot, at_y, lambda here, d: wy_slot(d))
+    table_sum(1)
+    table_relay(3)
+    wait_for(wy_in, 1, -1, 3, 4, 5)
     wy_sib = send(wy_recv.at[0], wy_recv.at[1], sibling)
-    table_relay(2)
-    table_sum(1)
+    table_sum(2)
+    low_sum()
+    table_pass()
 
     wy_sib.wait_recv()
     w_sum = wy_recv[0, 0]
@@ -532,17 +581,11 @@
         w_sum += wy_recv[0, d]
     for d in range(NY):
         w_sum += wy_recv[1, d]
-
-    def w_rows(place):
-        return gw_ref.at[pl.ds(pl.multiple_of(place * 8, 8), 8), :]
-
-    gw_ref[pl.ds(pl.multiple_of(dp * 8, 8), 8), :] = w_sum
-    w_back = {d: send(w_rows(dp), w_rows(dp), at_z(d)) for d in ARRIVE[1:]}
-
-    table_relay(3)
-    table_sum(2)
-    low_sum()
-    table_pass()
+    w_own[...] = w_sum
+    own_lanes = pl.ds(pl.multiple_of(core * B, B), B)
+    gw_ref[pl.ds(pl.multiple_of(dp * 8, 8), 8), own_lanes] = w_own[:, own_lanes]
+    w_back = {d: send(w_rows(0), w_rows(0), at_z(d)) for d in (2, -2, 1, -1)}
+
     table_sum(3)
     drain()
 
@@ -590,17 +633,15 @@
 
     to_near(0, 1)
 
-    wait_for(w_back, *ARRIVE[1:])
-    w_held = gw_ref.at[pl.ds(pl.multiple_of(x * 64, 64), 64), :]
-    for step in (2, 1, 3):
-        far_in.append(send(w_held, w_held, at_x(step)))
-
-
+    small_pass(w_back, w_rows, at_z, lambda here, d: w_rows(here))
     gather_pass(back, back_slot, at_z)
     to_near(1, 3)
     for copy in low_back:
         copy.wait_recv()
     low_back = gather_start(low_slot, at_z)
+    wait_for(w_back, 1, -1, 3, 4, 5)
+    w_held = gw_ref.at[pl.ds(pl.multiple_of(x * 64, 64), 64), pl.ds(pl.multiple_of(core * B, B), B)]
+    w_x = [send(w_held, w_held, at_x(step)) for step in (2, 1, 3)]
     to_far(0, 1)
     wait_for(back, 1, -1)
     to_near(3, 5)
@@ -620,6 +661,10 @@
             table_ref[pl.ds(pl.multiple_of(place, 32), 32), :] = l_back[p, far]
 
     to_far(5, 8)
+    for copy in w_x:
+        copy.wait_recv()
+    w_half = gw_ref.at[:, pl.ds(pl.multiple_of(core * B, B), B)]
+    far_in.append(send(w_half, w_half, sibling))
     for p, d in enumerate(ARRIVE):
         rows_of(x, p, d)
         rows_of(lax.rem(x + 1, NX), p, d)
@@ -678,20 +723,16 @@
             vmem(NZ, NX * B),
             vmem(16, B),
             vmem(NX, 16, B),
-            vmem(NZ, B, W, dtype=BF16),
-            vmem(2, B, W, dtype=BF16),
-            vmem(2, 64, W, dtype=BF16),
-            vmem(NZ, B, W, dtype=BF16),
-            vmem(3, B, W),
+            vmem(2, 4, 2, 64, W, dtype=BF16),
+            vmem(2, 4, 2, 64, W, dtype=BF16),
+            vmem(NZ, B, W),
             vmem(NX, B, W, dtype=BF16),
             vmem(NX, B, W, dtype=BF16),
             vmem(B, W),
             vmem(256, B),
-            vmem(B, 16 * B, dtype=BF16),
+            vmem(64, 16 * B, dtype=BF16),
             vmem(CAP, 16 * B, dtype=BF16),
-            vmem(B, CAP),
-            vmem(NY, 16, CAP),
-            vmem(NT, 8, CAP),
+            vmem(NT, 64, CAP, dtype=BF16),
             vmem(1152, NT * CAP, dtype=BF16),
             vmem(NT, 2 * B, CAP, dtype=BF16),
             vmem(NT, NX, 16, CAP, dtype=BF16),
@@ -700,8 +741,11 @@
             vmem(2 * B, W),
             vmem(NX, 64, W),
             vmem(64, W),
-            vmem(NZ, 8, W),
+            vmem(3, 8, W),
+            vmem(2, 8, W),
+            vmem(4, 8, W),
             vmem(2, NY, 8, W),
+            vmem(8, W),
             vmem(4, NX, E, 256),
             vmem(4, NX, E, 256, dtype=BF16),
             vmem(4, 2, 48, 256, dtype=BF16),

time: 92.5 us -> 91.7 us (level)
  the two profiles are of different devices: /device:TPU:4 before, /device:TPU:2 now
where the time goes in v3:
time: 91.7 us; the launch traced here: 91.5 us
  Pallas kernels  90.9 us (99%)
    pallas_call x1, Pallas kernels, on_device(): pl.pallas_call(kernel, out_shape=(jax.ShapeDtypeStruct((4096, E), BF16),...  89.4 us

profile of v3, /device:TPU:2, one launch (start us, length us, event | category | flops | bytes accessed | tf_op | source)
XLA Modules:
  0.0 91.5 jit_solution(15622388708873771961)
XLA Ops:
  0.6 89.4 %shard_map.112 = (bf16[4096,128]{1,0:T(8,128)(2,1)S(1)}, f32[256,256]{1,0:T(8,128)S(1)}) custom-call(bf16[128,256]{1,0:T(8,128)(2,1)} %q_ref.1, bf16[128,256]{1,0:T(8,128)(2,1)} %it_ref.1, bf16[128,128]{1,0:T(8,128)(2,1)} %pq_ref.1, bf16[128,128]{1,0:T(8,128)(2,1)} %pi_ref.1, bf16[128,256]{1,0:T(8,128)(2,1)} %wq_ref.1, bf16[128,256]{1,0:T(8,128)(2,1)} %wi_ref.1, ...), custom_call_target="tpu_custom_call" | custom-call | tf_op jit(solution)/shard_map/pallas_call | solution.py:702
  90.1 1.5 %shard_map.113 = (f32[4096,128]{1,0:T(8,128)}, f32[128,256]{1,0:T(8,128)}, f32[128,256]{1,0:T(8,128)}) custom-call(bf16[4096,128]{1,0:T(8,128)(2,1)S(1)} %get-tuple-element.5.table_ref, f32[256,256]{1,0:T(8,128)S(1)} %get-tuple-element.6.gw_ref), custom_call_target="tpu_custom_call" | custom-call | tf_op jit(solution)/shard_map/pallas_call | solution.py:783

commit v4 on v3

--- a/solution.py
+++ b/solution.py
@@ -302,7 +302,7 @@
     send_sum(1, 3, 0)
     source_row = iota((2 * B, CAP), 0)
     owner_row = iota((NT, CAP), 0)
-    low_row = lax.bitwise_and(iota((1152, CAP), 0), 1023)
+    low_row = iota((1024, CAP), 0)
 
     def one_hots(s, _):
         entry = lists[s].astype(F32)
@@ -313,14 +313,13 @@
         row = (high - 1) * 256 + low
         select[s] = (source == source_row).astype(BF16)
         lanes = pl.ds(pl.multiple_of(s * CAP, CAP), CAP)
-        onehot[:, lanes] = (lax.bitwise_and(row, 1023) == low_row).astype(BF16)
+        onehot[:, lanes] = (lax.bitwise_and(row - z * B, 1023) == low_row).astype(BF16)
         block = jnp.broadcast_to(lax.shift_right_arithmetic(row, 10), (16, CAP))
         for j in range(NX):
             factor[s, j] = (block == j).astype(BF16)
         return 0
 
     lax.fori_loop(0, 5, one_hots, 0)
-    lax.fori_loop(10, 13, one_hots, 0)
     send_sum(0, 3, 0)
     send_sum(1, 3, 1)
 
@@ -352,8 +351,7 @@
 
     for copy in list_sib:
         copy.wait_recv()
-    lax.fori_loop(5, 10, one_hots, 0)
-    lax.fori_loop(13, 16, one_hots, 0)
+    lax.fori_loop(5, 16, one_hots, 0)
     drain()
 
     item_grad = gi_own[0]
@@ -382,12 +380,14 @@
             values[j * E:(j + 1) * E, lanes] = got * jnp.tile(factor[s, j], (8, 1))
         return 0
 
-    def quarter_rows(p):
-        return pl.ds(pl.multiple_of(lax.rem(z + 4 + 3 * p * (p + 1), NZ) * B, B), 256)
-
-    def first_part(p, _):
-        part = dot(values[:, 0:FIRST], onehot[quarter_rows(p), 0:FIRST], NT_DIMS)
-        t_own[p] = part.reshape(NX, E, 256)
+    def two_blocks(b, columns):
+        rows = pl.ds(pl.multiple_of(b * 2 * E, 2 * E), 2 * E)
+        return dot(onehot[:, columns], values[rows, columns], NT_DIMS)
+
+    def first_part(b, _):
+        part = two_blocks(b, slice(0, FIRST))
+        for j in (0, 1):
+            t_own[2 * b + j] = part[:, j * E:(j + 1) * E].reshape(NZ, B, E)
         return 0
 
     gather_pass(pooled_in[1], pooled_slot(1), at_y)
@@ -400,6 +400,14 @@
         pooled_sib[1, low].wait_recv()
     lax.fori_loop(5, 10, place_values, 0)
 
+    lax.fori_loop(0, 1, first_part, 0)
+    wait_for(pooled_in[0], 3, -3, 4, -4)
+    to_sibling(0, 5, 8)
+    wait_for(pooled_in[1], 3, -3, 4, -4)
+    to_sibling(1, 5, 8)
+    lax.fori_loop(10, 13, place_values, 0)
+    lax.fori_loop(1, 2, first_part, 0)
+
     w_sum = w_part[pl.ds(pl.multiple_of(x * 64, 64), 64), :]
     for d in (1, 3, 2):
         w_in[d].wait_recv()
@@ -416,70 +424,65 @@
     ):
         wz_in[d] = send(wz_send.at[w_chunk(d), :], dst, at_z(via))
 
-    lax.fori_loop(0, 2, first_part, 0)
-    wait_for(pooled_in[0], 3, -3, 4, -4)
-    to_sibling(0, 5, 8)
-    wait_for(pooled_in[1], 3, -3, 4, -4)
-    to_sibling(1, 5, 8)
-    lax.fori_loop(10, 13, place_values, 0)
-    lax.fori_loop(2, 4, first_part, 0)
-    wait_for(wz_in, 4, 3, -3)
-    wz_pass[0] = wz_send[w_chunk(2), :] + wz_relay[0] + wz_relay[1]
-    wz_pass[1] = wz_send[w_chunk(-2), :] + wz_relay[2]
-    for side, d in ((0, 2), (1, -2)):
-        wz_in[d] = send(wz_pass.at[side], wz_recv.at[2 + side], at_z(d))
     pooled_sib[0, 5].wait_recv()
     pooled_sib[1, 5].wait_recv()
     lax.fori_loop(13, 16, place_values, 0)
 
+    bases = (4, 2, 6, 0)
     half_base = len(copies)
     copies.extend([None] * 8)
 
     def half_copy(p, side):
         return remote(
             half_base + 2 * p + side,
-            t_send.at[p, lax.rem(x + 2, NX), pl.ds(side * 48, 48), :],
+            t_send.at[lax.rem(x + 2, NX), pl.ds(bases[p], 2), pl.ds(side * 48, 48), :],
             tx_half.at[p, side],
             at_x(1 - 2 * side),
         )
 
-    def send_part(p, part):
-        part = t_own[p] + part.reshape(NX, E, 256)
-        t_own[p] = part
-        t_send[p] = part.astype(BF16)
-        half_copy(p, 0).start()
-        half_copy(p, 1).start()
-
-    def last_part(p, _):
-        send_part(p, dot(values[:, FIRST:], onehot[quarter_rows(p), FIRST:], NT_DIMS))
+    def last_part(i, _):
+        b = lax.rem(lax.div(x, 2) + 1 + i, 2)
+        part = two_blocks(b, slice(FIRST, NT * CAP))
+        for j in (0, 1):
+            block = t_own[2 * b + j] + part[:, j * E:(j + 1) * E].reshape(NZ, B, E)
+            t_own[2 * b + j] = block
+            t_send[2 * b + j] = block.astype(BF16)
+
+        @pl.when(i == 0)
+        def _():
+            for p in range(4):
+                for side in (0, 1):
+                    half_copy(p, side).start()
+
         return 0
 
-    lax.fori_loop(0, 4, last_part, 0)
+    lax.fori_loop(0, 2, last_part, 0)
     for p in range(4):
         for side in (0, 1):
             copies[half_base + 2 * p + side] = half_copy(p, side)
 
-    def low_columns(p, side):
-        return t_send.at[p, :, pl.ds(96, 32), pl.ds(side * B, B)]
+    def low_columns(d):
+        return t_send.at[:, d, pl.ds(96, 32), :]
 
     low_half = [
-        send(t_send.at[0, pl.ds(2 * side, 2), pl.ds(96, 32), pl.ds(0, B)], lz_half.at[side], at_z(2 - 4 * side))
+        send(t_send.at[pl.ds(2 * side, 2), 4, pl.ds(96, 32), :], lz_half.at[side], at_z(2 - 4 * side))
         for side in (0, 1)
     ]
     low_relay = [
-        send(low_columns(1, 1), lz_relay.at[0], at_z(1)),
-        send(low_columns(0, 1), lz_relay.at[1], at_z(-1)),
+        send(low_columns(3), lz_relay.at[0], at_z(1)),
+        send(low_columns(5), lz_relay.at[1], at_z(-1)),
     ]
     low_in = [
-        send(low_columns(3, 1), lz_recv.at[0], at_z(1)),
-        send(low_columns(2, 1), lz_recv.at[1], at_z(-1)),
+        send(low_columns(1), lz_recv.at[0], at_z(1)),
+        send(low_columns(7), lz_recv.at[1], at_z(-1)),
     ]
 
     def low_pass():
         for side in (0, 1):
             low_relay[side].wait_recv()
             low_half[side].wait_recv()
-            lz_own[side] = t_own[1 + side, :, 96:, 0:B] + lz_relay[side].astype(F32)
+            d = (2, 6)[side]
+            lz_own[side] = t_own[:, d, 96:, :] + lz_relay[side].astype(F32)
             pair_of = slice(2 * side, 2 * side + 2)
             lz_own[side, pair_of] += lz_half[side].astype(F32)
             lz_send[side] = lz_own[side].astype(BF16)
@@ -488,7 +491,7 @@
     low_x = {}
 
     def low_sum():
-        part = t_own[3, :, 96:, 0:B]
+        part = t_own[:, 0, 96:, :]
         for k in range(4):
             low_in[k].wait_recv()
             part += lz_recv[k].astype(F32)
@@ -505,26 +508,26 @@
             near = lax.rem(x + step + NX, NX)
             for half in (0, 1):
                 rows = slice(half * 48, half * 48 + 48)
-                part = t_own[p, near, rows, :]
+                part = t_own[near, bases[p]:bases[p] + 2, rows, :]
                 if half == side:
                     part += tx_half[p, side].astype(F32)
-                tx_relay[p, side, rows, :] = part.astype(BF16)
+                tx_relay[p, side, :, rows, :] = part.astype(BF16)
             relay_in[p, side] = send(tx_relay.at[p, side], tx_recv.at[p, side], at_x(step))
 
     def table_sum(p):
-        part = t_own[p, x, 0:96, :]
+        part = t_own[x, bases[p]:bases[p] + 2, 0:96, :]
         for side in (0, 1):
             relay_in[p, side].wait_recv()
             part += tx_recv[p, side].astype(F32)
-        tz_send[p] = part[:, B:].astype(BF16)
+        tz_send[p] = part[1].astype(BF16)
         if p == 0:
-            tz_first[...] = part[:, 0:B].astype(BF16)
+            tz_first[...] = part[0].astype(BF16)
             for side in (0, 1):
                 tz_half_in[side] = send(
                     tz_first.at[pl.ds(side * 48, 48), :], tz_half.at[side], at_z(2 - 4 * side)
                 )
         else:
-            tz_own[p - 1] = part[:, 0:B]
+            tz_own[p - 1] = part[0]
         if p < 2:
             tz_relay_in[1 - p] = send(tz_send.at[p], tz_relay.at[1 - p], at_z(2 * p - 1))
         else:
@@ -555,7 +558,14 @@
         return gw_ref.at[pl.ds(pl.multiple_of(place * 8, 8), 8), pl.ds(pl.multiple_of(core * B, B), B)]
 
     table_relay(0)
+    wait_for(wz_in, 4, 3, -3)
+    wz_pass[0] = wz_send[w_chunk(2), :] + wz_relay[0] + wz_relay[1]
+    wz_pass[1] = wz_send[w_chunk(-2), :] + wz_relay[2]
+    for side, d in ((0, 2), (1, -2)):
+        wz_in[d] = send(wz_pass.at[side], wz_recv.at[2 + side], at_z(d))
     table_relay(1)
+    table_sum(0)
+    low_pass()
     w_sum = wz_send[w_chunk(0), :]
     wait_for(wz_in, 1, -1, 2, -2)
     for k in range(4):
@@ -563,18 +573,17 @@
     wy_recv[0, 0] = w_sum
     wy_in = {d: send(wy_slot(0), wy_slot(d), at_y(d)) for d in (2, -2, 1, -1)}
 
-    table_sum(0)
-    low_pass()
     table_relay(2)
-    small_pass(wy_in, wy_slot, at_y, lambda here, d: wy_slot(d))
     table_sum(1)
     table_relay(3)
-    wait_for(wy_in, 1, -1, 3, 4, 5)
-    wy_sib = send(wy_recv.at[0], wy_recv.at[1], sibling)
+    small_pass(wy_in, wy_slot, at_y, lambda here, d: wy_slot(d))
     table_sum(2)
     low_sum()
     table_pass()
-
+    wait_for(wy_in, 1, -1, 3, 4, 5)
+    wy_sib = send(wy_recv.at[0], wy_recv.at[1], sibling)
+    table_sum(3)
+    drain()
     wy_sib.wait_recv()
     w_sum = wy_recv[0, 0]
     for d in range(1, NY):
@@ -586,8 +595,6 @@
     gw_ref[pl.ds(pl.multiple_of(dp * 8, 8), 8), own_lanes] = w_own[:, own_lanes]
     w_back = {d: send(w_rows(0), w_rows(0), at_z(d)) for d in (2, -2, 1, -1)}
 
-    table_sum(3)
-    drain()
 
     low = lz_own[2, x]
     for d in (1, 3, 2):
@@ -597,9 +604,8 @@
     for k in (1, 0, 2, 3):
         tz_in[k].wait_recv()
         part += tz_recv[k].astype(F32)
-    rows = jnp.concatenate([part, low], axis=0).T.astype(BF16)
-    t_back[x, 0] = rows[0:96]
-    l_back[0, x] = rows[96:]
+    t_back[x, 0] = part.astype(BF16)
+    l_back[0, x] = low.astype(BF16)
 
     def back_slot(d, half):
         if half is None:
@@ -633,18 +639,18 @@
 
     to_near(0, 1)
 
-    small_pass(w_back, w_rows, at_z, lambda here, d: w_rows(here))
     gather_pass(back, back_slot, at_z)
     to_near(1, 3)
     for copy in low_back:
         copy.wait_recv()
     low_back = gather_start(low_slot, at_z)
+    small_pass(w_back, w_rows, at_z, lambda here, d: w_rows(here))
+    to_far(0, 1)
+    wait_for(back, 1, -1)
+    to_near(3, 5)
     wait_for(w_back, 1, -1, 3, 4, 5)
     w_held = gw_ref.at[pl.ds(pl.multiple_of(x * 64, 64), 64), pl.ds(pl.multiple_of(core * B, B), B)]
     w_x = [send(w_held, w_held, at_x(step)) for step in (2, 1, 3)]
-    to_far(0, 1)
-    wait_for(back, 1, -1)
-    to_near(3, 5)
     to_far(1, 3)
     wait_for(back, 3, -3, 4, -4)
     to_near(5, 8)
@@ -733,7 +739,7 @@
             vmem(64, 16 * B, dtype=BF16),
             vmem(CAP, 16 * B, dtype=BF16),
             vmem(NT, 64, CAP, dtype=BF16),
-            vmem(1152, NT * CAP, dtype=BF16),
+            vmem(1024, NT * CAP, dtype=BF16),
             vmem(NT, 2 * B, CAP, dtype=BF16),
             vmem(NT, NX, 16, CAP, dtype=BF16),
             vmem(2, NT, E, B, dtype=BF16),
@@ -746,11 +752,11 @@
             vmem(4, 8, W),
             vmem(2, NY, 8, W),
             vmem(8, W),
-            vmem(4, NX, E, 256),
-            vmem(4, NX, E, 256, dtype=BF16),
-            vmem(4, 2, 48, 256, dtype=BF16),
-            vmem(4, 2, 96, 256, dtype=BF16),
-            vmem(4, 2, 96, 256, dtype=BF16),
+            vmem(NX, NZ, B, E),
+            vmem(NX, NZ, B, E, dtype=BF16),
+            vmem(4, 2, 2, 48, E, dtype=BF16),
+            vmem(4, 2, 2, 96, E, dtype=BF16),
+            vmem(4, 2, 2, 96, E, dtype=BF16),
             vmem(96, B, dtype=BF16),
             vmem(3, 96, B),
             vmem(4, 96, B, dtype=BF16),

time: 91.7 us -> 95.9 us (1.046)
  Pallas kernels: 90.9 us -> 95.1 us
    pallas_call x1, Pallas kernels: 89.4 us -> 93.6 us  [on_device(): pl.pallas_call(kernel, out_shape=(jax.ShapeDtypeStruct((4096, E), BF16),...]
where the time goes in v4:
time: 95.9 us; the launch traced here: 95.8 us
  Pallas kernels  95.1 us (99%)
    pallas_call x1, Pallas kernels, on_device(): pl.pallas_call(kernel, out_shape=(jax.ShapeDtypeStruct((4096, E), BF16),...  93.6 us

profile of v4, /device:TPU:2, one launch (start us, length us, event | category | flops | bytes accessed | tf_op | source)
XLA Modules:
  0.0 95.8 jit_solution(5544712581665600459)
XLA Ops:
  0.6 93.6 %shard_map.112 = (bf16[4096,128]{1,0:T(8,128)(2,1)S(1)}, f32[256,256]{1,0:T(8,128)S(1)}) custom-call(bf16[128,256]{1,0:T(8,128)(2,1)} %q_ref.1, bf16[128,256]{1,0:T(8,128)(2,1)} %it_ref.1, bf16[128,128]{1,0:T(8,128)(2,1)} %pq_ref.1, bf16[128,128]{1,0:T(8,128)(2,1)} %pi_ref.1, bf16[128,256]{1,0:T(8,128)(2,1)} %wq_ref.1, bf16[128,256]{1,0:T(8,128)(2,1)} %wi_ref.1, ...), custom_call_target="tpu_custom_call" | custom-call | tf_op jit(solution)/shard_map/pallas_call | solution.py:708
  94.3 1.5 %shard_map.113 = (f32[4096,128]{1,0:T(8,128)}, f32[128,256]{1,0:T(8,128)}, f32[128,256]{1,0:T(8,128)}) custom-call(bf16[4096,128]{1,0:T(8,128)(2,1)S(1)} %get-tuple-element.5.table_ref, f32[256,256]{1,0:T(8,128)S(1)} %get-tuple-element.6.gw_ref), custom_call_target="tpu_custom_call" | custom-call | tf_op jit(solution)/shard_map/pallas_call | solution.py:789

commit v5 on v3

--- a/solution.py
+++ b/solution.py
@@ -44,7 +44,7 @@
     ibuf, qbuf, ebuf, gbuf, tops, totals, st_send, st_recv,
     gi_send, gi_sum, gi_own, gq_send, gq_recv, gq_own,
     taken, slots_a, slots_b, lists, onehot, select, factor, pooled, values,
-    w_part, wx_recv, wz_send, wz_relay, wz_pass, wz_recv, wy_recv, w_own,
+    w_part, wx_recv, wz_send, wz_recv, wy_recv,
     t_own, t_send, tx_half, tx_relay, tx_recv, tz_first, tz_own, tz_send, tz_half, tz_relay, tz_back, tz_recv,
     lz_half, lz_relay, lz_own, lz_send, lz_recv, lx_send, lx_recv, t_back, l_back,
     load_sem, send_sem, recv_sem,
@@ -65,8 +65,8 @@
     sibling = (dp, tb + 1 - 2 * core)
     partners = (
         [at_x(d) for d in range(1, NX)]
-        + [at_z(d) for d in (1, 2, -1, -2)]
-        + [at_y(d) for d in (1, 2, -1, -2)]
+        + [at_z(d) for d in range(1, NZ)]
+        + [at_y(d) for d in range(1, NY)]
         + [sibling]
     )
     barrier = pltpu.get_barrier_semaphore()
@@ -320,7 +320,6 @@
         return 0
 
     lax.fori_loop(0, 5, one_hots, 0)
-    lax.fori_loop(10, 13, one_hots, 0)
     send_sum(0, 3, 0)
     send_sum(1, 3, 1)
 
@@ -352,8 +351,7 @@
 
     for copy in list_sib:
         copy.wait_recv()
-    lax.fori_loop(5, 10, one_hots, 0)
-    lax.fori_loop(13, 16, one_hots, 0)
+    lax.fori_loop(5, 16, one_hots, 0)
     drain()
 
     item_grad = gi_own[0]
@@ -400,34 +398,24 @@
         pooled_sib[1, low].wait_recv()
     lax.fori_loop(5, 10, place_values, 0)
 
-    w_sum = w_part[pl.ds(pl.multiple_of(x * 64, 64), 64), :]
-    for d in (1, 3, 2):
-        w_in[d].wait_recv()
-        w_sum += wx_recv[d]
-    wz_send[...] = w_sum
-
-    def w_chunk(d):
-        return pl.ds(pl.multiple_of(lax.rem(z + d + NZ, NZ) * 8, 8), 8)
-
-    wz_in = {}
-    for d, via, dst in (
-        (4, 2, wz_relay.at[0]), (3, 1, wz_relay.at[1]), (-3, -1, wz_relay.at[2]),
-        (1, 1, wz_recv.at[0]), (-1, -1, wz_recv.at[1]),
-    ):
-        wz_in[d] = send(wz_send.at[w_chunk(d), :], dst, at_z(via))
-
     lax.fori_loop(0, 2, first_part, 0)
     wait_for(pooled_in[0], 3, -3, 4, -4)
     to_sibling(0, 5, 8)
     wait_for(pooled_in[1], 3, -3, 4, -4)
     to_sibling(1, 5, 8)
     lax.fori_loop(10, 13, place_values, 0)
+
+    w_sum = w_part[pl.ds(pl.multiple_of(x * 64, 64), 64), :]
+    for d in (1, 3, 2):
+        w_in[d].wait_recv()
+        w_sum += wx_recv[d]
+    wz_send[...] = w_sum
+    wz_in = {}
+    for d in ARRIVE[1:]:
+        to_z = lax.rem(z + d, NZ)
+        wz_in[d] = send(wz_send.at[pl.ds(pl.multiple_of(to_z * 8, 8), 8), :], wz_recv.at[d], at_z(d))
+
     lax.fori_loop(2, 4, first_part, 0)
-    wait_for(wz_in, 4, 3, -3)
-    wz_pass[0] = wz_send[w_chunk(2), :] + wz_relay[0] + wz_relay[1]
-    wz_pass[1] = wz_send[w_chunk(-2), :] + wz_relay[2]
-    for side, d in ((0, 2), (1, -2)):
-        wz_in[d] = send(wz_pass.at[side], wz_recv.at[2 + side], at_z(d))
     pooled_sib[0, 5].wait_recv()
     pooled_sib[1, 5].wait_recv()
     lax.fori_loop(13, 16, place_values, 0)
@@ -540,40 +528,23 @@
             tz_back[side] = tz_own[side].astype(BF16)
             tz_in[2 + side] = send(tz_back.at[side], tz_recv.at[2 + side], at_z(2 - 4 * side))
 
-    def small_pass(got, slot, at, there):
-        got[2].wait_recv()
-        got[3] = send(slot(2), there(2, 3), at(1))
-        got[4] = send(slot(2), there(2, 4), at(2))
-        got[-2].wait_recv()
-        got[5] = send(slot(-2), there(-2, 5), at(-1))
-
-    def wy_slot(d):
-        return wy_recv.at[0, d % 8]
-
-    def w_rows(d):
-        place = x * NZ + lax.rem(z - d + NZ, NZ)
-        return gw_ref.at[pl.ds(pl.multiple_of(place * 8, 8), 8), pl.ds(pl.multiple_of(core * B, B), B)]
+    w_sum = wz_send[pl.ds(pl.multiple_of(z * 8, 8), 8), :]
+    for d in ARRIVE[1:]:
+        wz_in[d].wait_recv()
+        w_sum += wz_recv[d]
+    wy_recv[0, 0] = w_sum
+    wy_in = {d: send(wy_recv.at[0, 0], wy_recv.at[0, d], at_y(d)) for d in ARRIVE[1:]}
 
     table_relay(0)
     table_relay(1)
-    w_sum = wz_send[w_chunk(0), :]
-    wait_for(wz_in, 1, -1, 2, -2)
-    for k in range(4):
-        w_sum += wz_recv[k]
-    wy_recv[0, 0] = w_sum
-    wy_in = {d: send(wy_slot(0), wy_slot(d), at_y(d)) for d in (2, -2, 1, -1)}
-
     table_sum(0)
     low_pass()
+
+    for d in ARRIVE[1:]:
+        wy_in[d].wait_recv()
+    wy_sib = send(wy_recv.at[0], wy_recv.at[1], sibling)
     table_relay(2)
-    small_pass(wy_in, wy_slot, at_y, lambda here, d: wy_slot(d))
     table_sum(1)
-    table_relay(3)
-    wait_for(wy_in, 1, -1, 3, 4, 5)
-    wy_sib = send(wy_recv.at[0], wy_recv.at[1], sibling)
-    table_sum(2)
-    low_sum()
-    table_pass()
 
     wy_sib.wait_recv()
     w_sum = wy_recv[0, 0]
@@ -581,11 +552,14 @@
         w_sum += wy_recv[0, d]
     for d in range(NY):
         w_sum += wy_recv[1, d]
-    w_own[...] = w_sum
-    own_lanes = pl.ds(pl.multiple_of(core * B, B), B)
-    gw_ref[pl.ds(pl.multiple_of(dp * 8, 8), 8), own_lanes] = w_own[:, own_lanes]
-    w_back = {d: send(w_rows(0), w_rows(0), at_z(d)) for d in (2, -2, 1, -1)}
-
+    w_rows = gw_ref.at[pl.ds(pl.multiple_of(dp * 8, 8), 8), :]
+    gw_ref[pl.ds(pl.multiple_of(dp * 8, 8), 8), :] = w_sum
+    w_back = {d: send(w_rows, w_rows, at_z(d)) for d in ARRIVE[1:]}
+
+    table_relay(3)
+    table_sum(2)
+    low_sum()
+    table_pass()
     table_sum(3)
     drain()
 
@@ -633,15 +607,16 @@
 
     to_near(0, 1)
 
-    small_pass(w_back, w_rows, at_z, lambda here, d: w_rows(here))
+    wait_for(w_back, *ARRIVE[1:])
+    w_held = gw_ref.at[pl.ds(pl.multiple_of(x * 64, 64), 64), :]
+    for step in (2, 1, 3):
+        far_in.append(send(w_held, w_held, at_x(step)))
+
     gather_pass(back, back_slot, at_z)
     to_near(1, 3)
     for copy in low_back:
         copy.wait_recv()
     low_back = gather_start(low_slot, at_z)
-    wait_for(w_back, 1, -1, 3, 4, 5)
-    w_held = gw_ref.at[pl.ds(pl.multiple_of(x * 64, 64), 64), pl.ds(pl.multiple_of(core * B, B), B)]
-    w_x = [send(w_held, w_held, at_x(step)) for step in (2, 1, 3)]
     to_far(0, 1)
     wait_for(back, 1, -1)
     to_near(3, 5)
@@ -661,10 +636,6 @@
             table_ref[pl.ds(pl.multiple_of(place, 32), 32), :] = l_back[p, far]
 
     to_far(5, 8)
-    for copy in w_x:
-        copy.wait_recv()
-    w_half = gw_ref.at[:, pl.ds(pl.multiple_of(core * B, B), B)]
-    far_in.append(send(w_half, w_half, sibling))
     for p, d in enumerate(ARRIVE):
         rows_of(x, p, d)
         rows_of(lax.rem(x + 1, NX), p, d)
@@ -741,11 +712,8 @@
             vmem(2 * B, W),
             vmem(NX, 64, W),
             vmem(64, W),
-            vmem(3, 8, W),
-            vmem(2, 8, W),
-            vmem(4, 8, W),
+            vmem(NZ, 8, W),
             vmem(2, NY, 8, W),
-            vmem(8, W),
             vmem(4, NX, E, 256),
             vmem(4, NX, E, 256, dtype=BF16),
             vmem(4, 2, 48, 256, dtype=BF16),

time: 91.7 us -> 93.5 us (1.020)
  Pallas kernels: 90.9 us -> 92.8 us
    pallas_call x1, Pallas kernels: 89.4 us -> 91.3 us  [on_device(): pl.pallas_call(kernel, out_shape=(jax.ShapeDtypeStruct((4096, E), BF16),...]
where the time goes in v5:
time: 93.5 us; the launch traced here: 93.4 us
  Pallas kernels  92.8 us (99%)
    pallas_call x1, Pallas kernels, on_device(): pl.pallas_call(kernel, out_shape=(jax.ShapeDtypeStruct((4096, E), BF16),...  91.3 us

profile of v5, /device:TPU:2, one launch (start us, length us, event | category | flops | bytes accessed | tf_op | source)
XLA Modules:
  0.0 93.4 jit_solution(3854981363007698769)
XLA Ops:
  0.6 91.3 %shard_map.112 = (bf16[4096,128]{1,0:T(8,128)(2,1)S(1)}, f32[256,256]{1,0:T(8,128)S(1)}) custom-call(bf16[128,256]{1,0:T(8,128)(2,1)} %q_ref.1, bf16[128,256]{1,0:T(8,128)(2,1)} %it_ref.1, bf16[128,128]{1,0:T(8,128)(2,1)} %pq_ref.1, bf16[128,128]{1,0:T(8,128)(2,1)} %pi_ref.1, bf16[128,256]{1,0:T(8,128)(2,1)} %wq_ref.1, bf16[128,256]{1,0:T(8,128)(2,1)} %wi_ref.1, ...), custom_call_target="tpu_custom_call" | custom-call | tf_op jit(solution)/shard_map/pallas_call | solution.py:673
  91.9 1.5 %shard_map.113 = (f32[4096,128]{1,0:T(8,128)}, f32[128,256]{1,0:T(8,128)}, f32[128,256]{1,0:T(8,128)}) custom-call(bf16[4096,128]{1,0:T(8,128)(2,1)S(1)} %get-tuple-element.5.table_ref, f32[256,256]{1,0:T(8,128)S(1)} %get-tuple-element.6.gw_ref), custom_call_target="tpu_custom_call" | custom-call | tf_op jit(solution)/shard_map/pallas_call | solution.py:751

commit v6 on v3

--- a/solution.py
+++ b/solution.py
@@ -31,7 +31,6 @@
 
 ARRIVE = (0, 2, 6, 1, 7, 3, 5, 4)
 POS = {d: p for p, d in enumerate(ARRIVE)}
-RING = {d: p for p, d in enumerate((0, 1, 7, 2, 6, 3, 5, 4))}
 OWN = (0, 1, 2, 3, 4, 10, 11, 12)
 SIB = (5, 6, 7, 8, 9, 13, 14, 15)
 FIRST = 10 * CAP
@@ -42,7 +41,7 @@
     table_ref, gw_ref,
     pq, pi, wq, wi, pw, ow, rw,
     ibuf, qbuf, ebuf, gbuf, tops, totals, st_send, st_recv,
-    gi_send, gi_sum, gi_own, gq_send, gq_recv, gq_own,
+    gi_send, gi_relay, gi_half, gi_recv, gi_own, gq_send, gq_recv, gq_own,
     taken, slots_a, slots_b, lists, onehot, select, factor, pooled, values,
     w_part, wx_recv, wz_send, wz_relay, wz_pass, wz_recv, wy_recv, w_own,
     t_own, t_send, tx_half, tx_relay, tx_recv, tz_first, tz_own, tz_send, tz_half, tz_relay, tz_back, tz_recv,
@@ -129,24 +128,12 @@
         for name in names:
             got[name].wait_recv()
 
-    def item_half(d, half):
-        return ibuf.at[pl.ds(RING[d] * B + half * 64, 64), :]
-
-    item_in = {}
-    for up in (0, 1):
-        item_in[1, up] = send(it_ref.at[pl.ds(up * 64, 64), :], item_half(1, up), at_z(1))
-        item_in[7, 1 - up] = send(it_ref.at[pl.ds(64 - up * 64, 64), :], item_half(7, 1 - up), at_z(-1))
-
-    def item_step(k):
-        for up in (0, 1):
-            down = 1 - up
-            item_in[k, up].wait_recv()
-            if k < 3 or up == 0:
-                item_in[k + 1, up] = send(item_half(k, up), item_half(k + 1, up), at_z(1))
-            item_in[8 - k, down].wait_recv()
-            if k < 3 or down == 1:
-                item_in[7 - k, down] = send(item_half(8 - k, down), item_half(7 - k, down), at_z(-1))
-
+    def item_slot(d, half):
+        if half is None:
+            return ibuf.at[pl.ds(POS[d] * B, B), :]
+        return ibuf.at[pl.ds(POS[d] * B + half * 64, 64), :]
+
+    item_in = gather_start(item_slot, at_z, it_ref)
     query_in = {}
     for d in (1, 3, 2):
         query_in[d] = send(q_ref, qbuf.at[pl.ds(d * B, B), :], at_x(d))
@@ -163,7 +150,6 @@
         lax.shift_right_logical(at_col, 4) < lax.shift_right_logical(at_row, 4),
     ).astype(BF16)
     taken[...] = (counts[:, 0:B] + dot(earlier, counts[:, B:].astype(BF16))) * hits
-    item_step(1)
     list_row = iota((64, B), 0)
     list_owner, piece = lax.bitwise_and(list_row, 15), lax.shift_right_logical(list_row, 4)
     pair = iota((1, B), 1)
@@ -196,7 +182,7 @@
         return lists.at[OWN[POS[d]], pl.ds(half * 32, 32), :]
 
     list_in = gather_start(list_slot_of, at_y)
-    item_step(2)
+    gather_pass(item_in, item_slot, at_z)
 
     wait_for(query_in, 1, 3, 2)
 
@@ -210,11 +196,12 @@
         totals[pl.ds(p, 1), :] = jnp.sum(block, axis=0, keepdims=True)
         return 0
 
-    lax.fori_loop(0, 3, logits, 0)
-    item_step(3)
-    lax.fori_loop(3, 7, logits, 0)
-    wait_for(item_in, (4, 0), (4, 1))
-    lax.fori_loop(7, 8, logits, 0)
+    wait_for(item_in, 1, -1)
+    lax.fori_loop(0, 5, logits, 0, unroll=True)
+    wait_for(item_in, 3, -3)
+    lax.fori_loop(5, 7, logits, 0, unroll=True)
+    wait_for(item_in, 4, -4)
+    logits(7, 0)
 
     top = jnp.max(tops[...], axis=0, keepdims=True)
     total = jnp.sum(totals[...] * jnp.exp(tops[...] - top), axis=0, keepdims=True)
@@ -248,29 +235,27 @@
         gbuf[rows, :] = block
         return SCALE * dot(block, qbuf[...])
 
+    def far_terms(p, _):
+        gi_send[p] = item_terms(p).astype(BF16)
+        return 0
+
     def near_terms(p, _):
         gi_own[p] = item_terms(p)
         return 0
 
-    sum_in = {}
-    half_of = (slice(0, 64), slice(64, 128))
-
-    def send_sum(way, k, half):
-        p = RING[(4, 5, 6, 7)[k] if way == 0 else (4, 3, 2, 1)[k]]
-        block = gi_own[p, half_of[half], :]
-        if (way, k - 1, half) in sum_in:
-            sum_in[way, k - 1, half].wait_recv()
-            block += gi_sum[way, k - 1, half].astype(F32)
-        gi_send[way, k, half] = block.astype(BF16)
-        sum_in[way, k, half] = send(gi_send.at[way, k, half], gi_sum.at[way, k, half], at_z(1 - 2 * way))
-
-    near_terms(7, 0)
-    send_sum(0, 0, 0)
-    send_sum(1, 0, 1)
-    lax.fori_loop(5, 7, near_terms, 0)
-    send_sum(0, 1, 1)
-    send_sum(1, 1, 0)
-    lax.fori_loop(0, 5, near_terms, 0)
+    far_terms(7, 0)
+    half_in = [
+        send(gi_send.at[7, pl.ds(0, 64), :], gi_half.at[0], at_z(2)),
+        send(gi_send.at[7, pl.ds(64, 64), :], gi_half.at[1], at_z(-2)),
+    ]
+    lax.fori_loop(5, 7, far_terms, 0, unroll=True)
+    relay_in = [
+        send(gi_send.at[POS[5]], gi_relay.at[0], at_z(1)),
+        send(gi_send.at[POS[3]], gi_relay.at[1], at_z(-1)),
+    ]
+    lax.fori_loop(3, 5, far_terms, 0, unroll=True)
+    grad_in = {d: send(gi_send.at[POS[d]], gi_recv.at[POS[d]], at_z(-d)) for d in (7, 1)}
+    lax.fori_loop(0, 3, near_terms, 0, unroll=True)
     same = iota((B, B), 0) == iota((B, B), 1)
     diagonal = ebuf[0:B, 0:B] * totals[0:1, 0:B] - jnp.where(same, weight, 0.0)
     gbuf[0:B, 0:B] = diagonal.astype(BF16)
@@ -281,10 +266,14 @@
     for k in range(1, NX):
         gq_send[k] = terms[k * B:(k + 1) * B, :].astype(BF16)
     query_grad_in = {k: send(gq_send.at[k], gq_recv.at[k], at_x(-k)) for k in (2, 1, 3)}
-    send_sum(0, 1, 0)
-    send_sum(1, 1, 1)
-    send_sum(0, 2, 1)
-    send_sum(1, 2, 0)
+    for side, (d, rows) in enumerate(((6, slice(0, 64)), (2, slice(64, 128)))):
+        p = POS[d]
+        relay_in[side].wait_recv()
+        half_in[side].wait_recv()
+        gi_own[p] += gi_relay[side].astype(F32)
+        gi_own[p, rows, :] += gi_half[side].astype(F32)
+        gi_send[p] = gi_own[p].astype(BF16)
+        grad_in[d] = send(gi_send.at[p], gi_recv.at[p], at_z(-d))
 
     list_sib = []
 
@@ -296,10 +285,6 @@
     wait_for(list_in, 1, -1, 3, -3, 4, -4)
     lists_to_sibling(0, 5)
     lists_to_sibling(5, 8)
-    send_sum(0, 2, 0)
-    send_sum(1, 2, 1)
-    send_sum(0, 3, 1)
-    send_sum(1, 3, 0)
     source_row = iota((2 * B, CAP), 0)
     owner_row = iota((NT, CAP), 0)
     low_row = lax.bitwise_and(iota((1152, CAP), 0), 1023)
@@ -321,8 +306,6 @@
 
     lax.fori_loop(0, 5, one_hots, 0)
     lax.fori_loop(10, 13, one_hots, 0)
-    send_sum(0, 3, 0)
-    send_sum(1, 3, 1)
 
     query_grad = gq_own[...]
     for k in (1, 3, 2):
@@ -357,10 +340,9 @@
     drain()
 
     item_grad = gi_own[0]
-    for way in (0, 1):
-        for half in (0, 1):
-            sum_in[way, 3, half].wait_recv()
-        item_grad += gi_sum[way, 3].reshape(B, W).astype(F32)
+    for d in (1, 7, 2, 6):
+        grad_in[d].wait_recv()
+        item_grad += gi_recv[POS[d]].astype(F32)
     item_grad = item_grad.astype(BF16)
     pooled[1, 0] = dot(wi[...], item_grad, NT_DIMS).astype(BF16)
     pooled_in[1] = gather_start(pooled_slot(1), at_y)
@@ -394,11 +376,11 @@
     wait_for(pooled_in[1], 1, -1)
     to_sibling(1, 1, 3)
     to_sibling(1, 3, 5)
-    lax.fori_loop(0, 5, place_values, 0)
+    lax.fori_loop(0, 5, place_values, 0, unroll=True)
     for low in (0, 1, 3):
         pooled_sib[0, low].wait_recv()
         pooled_sib[1, low].wait_recv()
-    lax.fori_loop(5, 10, place_values, 0)
+    lax.fori_loop(5, 10, place_values, 0, unroll=True)
 
     w_sum = w_part[pl.ds(pl.multiple_of(x * 64, 64), 64), :]
     for d in (1, 3, 2):
@@ -421,7 +403,7 @@
     to_sibling(0, 5, 8)
     wait_for(pooled_in[1], 3, -3, 4, -4)
     to_sibling(1, 5, 8)
-    lax.fori_loop(10, 13, place_values, 0)
+    lax.fori_loop(10, 13, place_values, 0, unroll=True)
     lax.fori_loop(2, 4, first_part, 0)
     wait_for(wz_in, 4, 3, -3)
     wz_pass[0] = wz_send[w_chunk(2), :] + wz_relay[0] + wz_relay[1]
@@ -430,7 +412,7 @@
         wz_in[d] = send(wz_pass.at[side], wz_recv.at[2 + side], at_z(d))
     pooled_sib[0, 5].wait_recv()
     pooled_sib[1, 5].wait_recv()
-    lax.fori_loop(13, 16, place_values, 0)
+    lax.fori_loop(13, 16, place_values, 0, unroll=True)
 
     half_base = len(copies)
     copies.extend([None] * 8)
@@ -723,9 +705,11 @@
             vmem(NZ, NX * B),
             vmem(16, B),
             vmem(NX, 16, B),
-            vmem(2, 4, 2, 64, W, dtype=BF16),
-            vmem(2, 4, 2, 64, W, dtype=BF16),
-            vmem(NZ, B, W),
+            vmem(NZ, B, W, dtype=BF16),
+            vmem(2, B, W, dtype=BF16),
+            vmem(2, 64, W, dtype=BF16),
+            vmem(NZ, B, W, dtype=BF16),
+            vmem(3, B, W),
             vmem(NX, B, W, dtype=BF16),
             vmem(NX, B, W, dtype=BF16),
             vmem(B, W),

time: 91.7 us -> 85.7 us (0.935)
  Pallas kernels: 90.9 us -> 84.9 us
    pallas_call x1, Pallas kernels: 89.4 us -> 83.4 us  [on_device(): pl.pallas_call(kernel, out_shape=(jax.ShapeDtypeStruct((4096, E), BF16),...]
where the time goes in v6:
time: 85.7 us; the launch traced here: 85.6 us
  Pallas kernels  84.9 us (99%)
    pallas_call x1, Pallas kernels, on_device(): pl.pallas_call(kernel, out_shape=(jax.ShapeDtypeStruct((4096, E), BF16),...  83.4 us

profile of v6, /device:TPU:2, one launch (start us, length us, event | category | flops | bytes accessed | tf_op | source)
XLA Modules:
  0.0 85.6 jit_solution(8569826249433494576)
XLA Ops:
  0.6 83.4 %shard_map.112 = (bf16[4096,128]{1,0:T(8,128)(2,1)S(1)}, f32[256,256]{1,0:T(8,128)S(1)}) custom-call(bf16[128,256]{1,0:T(8,128)(2,1)} %q_ref.1, bf16[128,256]{1,0:T(8,128)(2,1)} %it_ref.1, bf16[128,128]{1,0:T(8,128)(2,1)} %pq_ref.1, bf16[128,128]{1,0:T(8,128)(2,1)} %pi_ref.1, bf16[128,256]{1,0:T(8,128)(2,1)} %wq_ref.1, bf16[128,256]{1,0:T(8,128)(2,1)} %wi_ref.1, ...), custom_call_target="tpu_custom_call" | custom-call | tf_op jit(solution)/shard_map/pallas_call | solution.py:684
  84.1 1.5 %shard_map.113 = (f32[4096,128]{1,0:T(8,128)}, f32[128,256]{1,0:T(8,128)}, f32[128,256]{1,0:T(8,128)}) custom-call(bf16[4096,128]{1,0:T(8,128)(2,1)S(1)} %get-tuple-element.5.table_ref, f32[256,256]{1,0:T(8,128)S(1)} %get-tuple-element.6.gw_ref), custom_call_target="tpu_custom_call" | custom-call | tf_op jit(solution)/shard_map/pallas_call | solution.py:767

commit v7 on v6

--- a/solution.py
+++ b/solution.py
@@ -173,7 +173,7 @@
         slots_a[:, lanes] = jnp.where(list_owner == owner, part, 0).astype(F32).astype(BF16)
         return 0
 
-    lax.fori_loop(0, 16, list_slot, 0)
+    lax.fori_loop(0, 16, list_slot, 0, unroll=True)
     lists[0] = dot(slots_a[...], slots_b[...], NT_DIMS).astype(BF16)
 
     def list_slot_of(d, half):
@@ -287,7 +287,7 @@
     lists_to_sibling(5, 8)
     source_row = iota((2 * B, CAP), 0)
     owner_row = iota((NT, CAP), 0)
-    low_row = lax.bitwise_and(iota((1152, CAP), 0), 1023)
+    low_row = iota((1024, CAP), 0)
 
     def one_hots(s, _):
         entry = lists[s].astype(F32)
@@ -298,14 +298,14 @@
         row = (high - 1) * 256 + low
         select[s] = (source == source_row).astype(BF16)
         lanes = pl.ds(pl.multiple_of(s * CAP, CAP), CAP)
-        onehot[:, lanes] = (lax.bitwise_and(row, 1023) == low_row).astype(BF16)
+        onehot[:, lanes] = (lax.bitwise_and(row - z * B, 1023) == low_row).astype(BF16)
         block = jnp.broadcast_to(lax.shift_right_arithmetic(row, 10), (16, CAP))
         for j in range(NX):
             factor[s, j] = (block == j).astype(BF16)
         return 0
 
-    lax.fori_loop(0, 5, one_hots, 0)
-    lax.fori_loop(10, 13, one_hots, 0)
+    lax.fori_loop(0, 5, one_hots, 0, unroll=True)
+    lax.fori_loop(10, 13, one_hots, 0, unroll=True)
 
     query_grad = gq_own[...]
     for k in (1, 3, 2):
@@ -335,8 +335,8 @@
 
     for copy in list_sib:
         copy.wait_recv()
-    lax.fori_loop(5, 10, one_hots, 0)
-    lax.fori_loop(13, 16, one_hots, 0)
+    lax.fori_loop(5, 10, one_hots, 0, unroll=True)
+    lax.fori_loop(13, 16, one_hots, 0, unroll=True)
     drain()
 
     item_grad = gi_own[0]
@@ -365,7 +365,7 @@
         return 0
 
     def quarter_rows(p):
-        return pl.ds(pl.multiple_of(lax.rem(z + 4 + 3 * p * (p + 1), NZ) * B, B), 256)
+        return pl.ds(pl.multiple_of(lax.rem(4 + 3 * p * (p + 1), NZ) * B, B), 256)
 
     def first_part(p, _):
         part = dot(values[:, 0:FIRST], onehot[quarter_rows(p), 0:FIRST], NT_DIMS)
@@ -717,7 +717,7 @@
             vmem(64, 16 * B, dtype=BF16),
             vmem(CAP, 16 * B, dtype=BF16),
             vmem(NT, 64, CAP, dtype=BF16),
-            vmem(1152, NT * CAP, dtype=BF16),
+            vmem(1024, NT * CAP, dtype=BF16),
             vmem(NT, 2 * B, CAP, dtype=BF16),
             vmem(NT, NX, 16, CAP, dtype=BF16),
             vmem(2, NT, E, B, dtype=BF16),

time: 85.7 us -> 86.7 us (1.012)
  the two profiles are of different devices: /device:TPU:2 before, /device:TPU:4 now
where the time goes in v7:
time: 86.7 us; the launch traced here: 86.5 us
  Pallas kernels  85.9 us (99%)
    pallas_call x1, Pallas kernels, on_device(): pl.pallas_call(kernel, out_shape=(jax.ShapeDtypeStruct((4096, E), BF16),...  84.4 us

profile of v7, /device:TPU:4, one launch (start us, length us, event | category | flops | bytes accessed | tf_op | source)
XLA Modules:
  0.0 86.5 jit_solution(9431630937532985528)
XLA Ops:
  0.6 84.4 %shard_map.112 = (bf16[4096,128]{1,0:T(8,128)(2,1)S(1)}, f32[256,256]{1,0:T(8,128)S(1)}) custom-call(bf16[128,256]{1,0:T(8,128)(2,1)} %q_ref.1, bf16[128,256]{1,0:T(8,128)(2,1)} %it_ref.1, bf16[128,128]{1,0:T(8,128)(2,1)} %pq_ref.1, bf16[128,128]{1,0:T(8,128)(2,1)} %pi_ref.1, bf16[128,256]{1,0:T(8,128)(2,1)} %wq_ref.1, bf16[128,256]{1,0:T(8,128)(2,1)} %wi_ref.1, ...), custom_call_target="tpu_custom_call" | custom-call | tf_op jit(solution)/shard_map/pallas_call | solution.py:684
  85.0 1.5 %shard_map.113 = (f32[4096,128]{1,0:T(8,128)}, f32[128,256]{1,0:T(8,128)}, f32[128,256]{1,0:T(8,128)}) custom-call(bf16[4096,128]{1,0:T(8,128)(2,1)S(1)} %get-tuple-element.5.table_ref, f32[256,256]{1,0:T(8,128)S(1)} %get-tuple-element.6.gw_ref), custom_call_target="tpu_custom_call" | custom-call | tf_op jit(solution)/shard_map/pallas_call | solution.py:767

commit v8 on v7

--- a/solution.py
+++ b/solution.py
@@ -304,8 +304,8 @@
             factor[s, j] = (block == j).astype(BF16)
         return 0
 
-    lax.fori_loop(0, 5, one_hots, 0, unroll=True)
-    lax.fori_loop(10, 13, one_hots, 0, unroll=True)
+    lax.fori_loop(0, 5, one_hots, 0)
+    lax.fori_loop(10, 13, one_hots, 0)
 
     query_grad = gq_own[...]
     for k in (1, 3, 2):
@@ -335,8 +335,8 @@
 
     for copy in list_sib:
         copy.wait_recv()
-    lax.fori_loop(5, 10, one_hots, 0, unroll=True)
-    lax.fori_loop(13, 16, one_hots, 0, unroll=True)
+    lax.fori_loop(5, 10, one_hots, 0)
+    lax.fori_loop(13, 16, one_hots, 0)
     drain()
 
     item_grad = gi_own[0]
@@ -398,13 +398,13 @@
     ):
         wz_in[d] = send(wz_send.at[w_chunk(d), :], dst, at_z(via))
 
-    lax.fori_loop(0, 2, first_part, 0)
+    lax.fori_loop(0, 2, first_part, 0, unroll=True)
     wait_for(pooled_in[0], 3, -3, 4, -4)
     to_sibling(0, 5, 8)
     wait_for(pooled_in[1], 3, -3, 4, -4)
     to_sibling(1, 5, 8)
     lax.fori_loop(10, 13, place_values, 0, unroll=True)
-    lax.fori_loop(2, 4, first_part, 0)
+    lax.fori_loop(2, 4, first_part, 0, unroll=True)
     wait_for(wz_in, 4, 3, -3)
     wz_pass[0] = wz_send[w_chunk(2), :] + wz_relay[0] + wz_relay[1]
     wz_pass[1] = wz_send[w_chunk(-2), :] + wz_relay[2]
@@ -436,7 +436,7 @@
         send_part(p, dot(values[:, FIRST:], onehot[quarter_rows(p), FIRST:], NT_DIMS))
         return 0
 
-    lax.fori_loop(0, 4, last_part, 0)
+    lax.fori_loop(0, 4, last_part, 0, unroll=True)
     for p in range(4):
         for side in (0, 1):
             copies[half_base + 2 * p + side] = half_copy(p, side)

time: 86.7 us -> 86.8 us (level)
  no operation moved by 1% of the time
where the time goes in v8:
time: 86.8 us; the launch traced here: 86.6 us
  Pallas kernels  86 us (99%)
    pallas_call x1, Pallas kernels, on_device(): pl.pallas_call(kernel, out_shape=(jax.ShapeDtypeStruct((4096, E), BF16),...  84.5 us

profile of v8, /device:TPU:4, one launch (start us, length us, event | category | flops | bytes accessed | tf_op | source)
XLA Modules:
  0.0 86.6 jit_solution(13864373286669211430)
XLA Ops:
  0.6 84.5 %shard_map.112 = (bf16[4096,128]{1,0:T(8,128)(2,1)S(1)}, f32[256,256]{1,0:T(8,128)S(1)}) custom-call(bf16[128,256]{1,0:T(8,128)(2,1)} %q_ref.1, bf16[128,256]{1,0:T(8,128)(2,1)} %it_ref.1, bf16[128,128]{1,0:T(8,128)(2,1)} %pq_ref.1, bf16[128,128]{1,0:T(8,128)(2,1)} %pi_ref.1, bf16[128,256]{1,0:T(8,128)(2,1)} %wq_ref.1, bf16[128,256]{1,0:T(8,128)(2,1)} %wi_ref.1, ...), custom_call_target="tpu_custom_call" | custom-call | tf_op jit(solution)/shard_map/pallas_call | solution.py:684
  85.1 1.5 %shard_map.113 = (f32[4096,128]{1,0:T(8,128)}, f32[128,256]{1,0:T(8,128)}, f32[128,256]{1,0:T(8,128)}) custom-call(bf16[4096,128]{1,0:T(8,128)(2,1)S(1)} %get-tuple-element.5.table_ref, f32[256,256]{1,0:T(8,128)S(1)} %get-tuple-element.6.gw_ref), custom_call_target="tpu_custom_call" | custom-call | tf_op jit(solution)/shard_map/pallas_call | solution.py:767

commit v9 on v6

--- a/solution.py
+++ b/solution.py
@@ -382,6 +382,12 @@
         pooled_sib[1, low].wait_recv()
     lax.fori_loop(5, 10, place_values, 0, unroll=True)
 
+    lax.fori_loop(0, 2, first_part, 0)
+    wait_for(pooled_in[0], 3, -3, 4, -4)
+    to_sibling(0, 5, 8)
+    wait_for(pooled_in[1], 3, -3, 4, -4)
+    to_sibling(1, 5, 8)
+    lax.fori_loop(10, 13, place_values, 0, unroll=True)
     w_sum = w_part[pl.ds(pl.multiple_of(x * 64, 64), 64), :]
     for d in (1, 3, 2):
         w_in[d].wait_recv()
@@ -398,18 +404,7 @@
     ):
         wz_in[d] = send(wz_send.at[w_chunk(d), :], dst, at_z(via))
 
-    lax.fori_loop(0, 2, first_part, 0)
-    wait_for(pooled_in[0], 3, -3, 4, -4)
-    to_sibling(0, 5, 8)
-    wait_for(pooled_in[1], 3, -3, 4, -4)
-    to_sibling(1, 5, 8)
-    lax.fori_loop(10, 13, place_values, 0, unroll=True)
     lax.fori_loop(2, 4, first_part, 0)
-    wait_for(wz_in, 4, 3, -3)
-    wz_pass[0] = wz_send[w_chunk(2), :] + wz_relay[0] + wz_relay[1]
-    wz_pass[1] = wz_send[w_chunk(-2), :] + wz_relay[2]
-    for side, d in ((0, 2), (1, -2)):
-        wz_in[d] = send(wz_pass.at[side], wz_recv.at[2 + side], at_z(d))
     pooled_sib[0, 5].wait_recv()
     pooled_sib[1, 5].wait_recv()
     lax.fori_loop(13, 16, place_values, 0, unroll=True)
@@ -521,6 +516,12 @@
             tz_own[side, rows, :] += tz_half[side].astype(F32)
             tz_back[side] = tz_own[side].astype(BF16)
             tz_in[2 + side] = send(tz_back.at[side], tz_recv.at[2 + side], at_z(2 - 4 * side))
+
+    wait_for(wz_in, 4, 3, -3)
+    wz_pass[0] = wz_send[w_chunk(2), :] + wz_relay[0] + wz_relay[1]
+    wz_pass[1] = wz_send[w_chunk(-2), :] + wz_relay[2]
+    for side, d in ((0, 2), (1, -2)):
+        wz_in[d] = send(wz_pass.at[side], wz_recv.at[2 + side], at_z(d))
 
     def small_pass(got, slot, at, there):
         got[2].wait_recv()

time: 85.7 us -> 88.2 us (1.029)
  the two profiles are of different devices: /device:TPU:2 before, /device:TPU:4 now
where the time goes in v9:
time: 88.2 us; the launch traced here: 88 us
  Pallas kernels  87.4 us (99%)
    pallas_call x1, Pallas kernels, on_device(): pl.pallas_call(kernel, out_shape=(jax.ShapeDtypeStruct((4096, E), BF16),...  85.9 us

profile of v9, /device:TPU:4, one launch (start us, length us, event | category | flops | bytes accessed | tf_op | source)
XLA Modules:
  0.0 88.0 jit_solution(17554839302519681938)
XLA Ops:
  0.6 85.9 %shard_map.112 = (bf16[4096,128]{1,0:T(8,128)(2,1)S(1)}, f32[256,256]{1,0:T(8,128)S(1)}) custom-call(bf16[128,256]{1,0:T(8,128)(2,1)} %q_ref.1, bf16[128,256]{1,0:T(8,128)(2,1)} %it_ref.1, bf16[128,128]{1,0:T(8,128)(2,1)} %pq_ref.1, bf16[128,128]{1,0:T(8,128)(2,1)} %pi_ref.1, bf16[128,256]{1,0:T(8,128)(2,1)} %wq_ref.1, bf16[128,256]{1,0:T(8,128)(2,1)} %wi_ref.1, ...), custom_call_target="tpu_custom_call" | custom-call | tf_op jit(solution)/shard_map/pallas_call | solution.py:685
  86.6 1.5 %shard_map.113 = (f32[4096,128]{1,0:T(8,128)}, f32[128,256]{1,0:T(8,128)}, f32[128,256]{1,0:T(8,128)}) custom-call(bf16[4096,128]{1,0:T(8,128)(2,1)S(1)} %get-tuple-element.5.table_ref, f32[256,256]{1,0:T(8,128)S(1)} %get-tuple-element.6.gw_ref), custom_call_target="tpu_custom_call" | custom-call | tf_op jit(solution)/shard_map/pallas_call | solution.py:768
